TPU v7x, 256 devices: a whole 4x4x8 slice. The times are simulated.
256 devices in a mesh: fsdp: 16 (over z_lo, y), grp: 4 (over x), tp: 4 (over z_hi, core).
Axes of the slice: x: 4, y: 4, z: 8 (z_hi: 2, z_lo: 4; z = z_hi * 4 + z_lo), core: 2. Of those that a mesh axis runs over, the one named last changes fastest.
Arguments:
- learner_input: bfloat16 [16384, 5120], P('fsdp', 'grp'), may hold values from -6 to 6
- cotangent: bfloat16 [16384, 5120], P('fsdp', 'tp'), may hold values from -6 to 6
- token_ids: int32 [16384], P('fsdp'), may hold values from 0 to 261119, as said below
- rewards: float32 [64], replicated, may hold values from -6 to 6
- group_ids: int32 [64], replicated, may hold values from 0 to 15, never falling along the last dimension, each value on 1 to 8 neighbouring positions
- weight_master: float32 [5120, 5120], P(('tp', 'fsdp'), 'grp'), may hold values from -0.078125 to 0.078125
- adam_first: float32 [5120, 5120], P(('tp', 'fsdp'), 'grp'), may hold values from -6 to 6
- adam_second: float32 [5120, 5120], P(('tp', 'fsdp'), 'grp'), may hold values from 0.01 to 1
- hidden_rows: bfloat16 [128, 5120], P(('fsdp', 'grp')), may hold values from -6 to 6
- cache_keys: bfloat16 [128, 128, 5120], P(('fsdp', 'grp'), None, 'tp'), may hold values from -360 to 360
- cache_values: bfloat16 [128, 128, 5120], P(('fsdp', 'grp'), None, 'tp'), may hold values from -6 to 6
- cache_lengths: int32 [128], P(('fsdp', 'grp')), may hold values from 1 to 128, as said below
- ssm_state: float32 [128, 128, 5120], P(('fsdp', 'grp'), None, 'tp'), may hold values from -6 to 6
- state_weight: bfloat16 [5120, 256], replicated, may hold values from -0.0078125 to 0.0078125
- decay_rate: float32 [5120], P('tp'), may hold values from 0.05 to 4
Outputs:
- new_weight: float32 [5120, 5120], P(('tp', 'fsdp'), 'grp')
- new_first: float32 [5120, 5120], P(('tp', 'fsdp'), 'grp')
- new_second: float32 [5120, 5120], P(('tp', 'fsdp'), 'grp')
- decoded: bfloat16 [128, 5120], P(('fsdp', 'grp'))
Inputs may be any that keep to these rules, and one draw needn't show every extreme that they name: `token_ids`: each sequence of 256 ids holds nonzero ids on a prefix of 128 or more positions and 0 after it. `cache_lengths`: among the 2 rows of each replica one has exactly 128 live positions.
All inputs are finite; a program needn't handle non-finite values.
Results may differ from a plain program's by a relative error of at most 0.033.
Values may be sent and summed in bfloat16 or wider, within the bound.
A program may use at most 128 MiB of HBM per device.

v0:
```python
import math

import jax
import jax.numpy as jnp
from jax import lax
from jax.sharding import PartitionSpec as P

HEAD = 128
NST = 128
SEQ = 256
STEPS = 4


beta_one = 0.9
beta_two = 0.95
learn_rate = 0.001
weight_decay = 0.1
adam_eps = 1e-08
adam_step = 10.0
norm_eps = 1e-05
mask_fill = -1e30


def group_advantage(rewards, group_ids):
    same_group = (group_ids[:, None] == group_ids[None, :]).astype(jnp.float32)
    group_total = jnp.sum(same_group * rewards[None, :], axis=1)
    group_count = jnp.sum(same_group, axis=1)
    return rewards - group_total / group_count


def attend(query_bf, key_heads, value_heads, valid_mask, own_keys, step_index):
    row_total, local_width = query_bf.shape
    head_count = key_heads.shape[2]
    query_heads = query_bf.reshape(row_total, head_count, HEAD)
    own_heads = own_keys.reshape(row_total, STEPS, head_count, HEAD)
    score_scale = 1.0 / math.sqrt(HEAD)
    cache_scores = (
        jnp.einsum("rhd,rlhd->rhl", query_heads, key_heads, preferred_element_type=jnp.float32)
        * score_scale
    )
    own_scores = (
        jnp.einsum("rhd,rshd->rhs", query_heads, own_heads, preferred_element_type=jnp.float32)
        * score_scale
    )
    own_valid = (jnp.arange(STEPS) <= step_index)[None, None, :]
    cache_valid = valid_mask[:, None, :]
    cache_scores = jnp.where(cache_valid, cache_scores, mask_fill)
    own_scores = jnp.where(own_valid, own_scores, mask_fill)
    score_top = jnp.maximum(jnp.max(cache_scores, axis=2), jnp.max(own_scores, axis=2))[:, :, None]
    cache_exp = jnp.where(cache_valid, jnp.exp(cache_scores - score_top), 0.0)
    own_exp = jnp.where(own_valid, jnp.exp(own_scores - score_top), 0.0)
    exp_total = jnp.sum(cache_exp, axis=2, keepdims=True) + jnp.sum(own_exp, axis=2, keepdims=True)
    cache_prob = (cache_exp / exp_total).astype(jnp.bfloat16)
    own_prob = (own_exp / exp_total).astype(jnp.bfloat16)
    attended = jnp.einsum(
        "rhl,rlhd->rhd", cache_prob, value_heads, preferred_element_type=jnp.float32
    )
    attended = attended + jnp.einsum(
        "rhs,rshd->rhd", own_prob, own_heads, preferred_element_type=jnp.float32
    )
    return attended.reshape(row_total, local_width)


def ssm_update(query_vals, normed, ssm_carry, state_weight, decay_rate):
    gate_vals = jnp.dot(normed, state_weight, preferred_element_type=jnp.float32)
    in_gate = gate_vals[:, :NST]
    out_gate = gate_vals[:, NST:]
    step_size = jax.nn.softplus(query_vals)
    decay_step = jnp.exp(-decay_rate[None, :] * step_size)
    ssm_carry = (
        decay_step[:, None, :] * ssm_carry
        + in_gate[:, :, None] * (step_size * query_vals)[:, None, :]
    )
    ssm_out = jnp.einsum("rk,rkc->rc", out_gate, ssm_carry, precision=lax.Precision.HIGHEST)
    return (ssm_out, ssm_carry)


def decode_rows(
    hidden_rows,
    cache_keys,
    cache_values,
    cache_lengths,
    ssm_state,
    state_weight,
    decay_rate,
    project_query,
    project_output,
):
    row_total, cache_size, local_width = cache_keys.shape
    head_count = local_width // HEAD
    key_heads = cache_keys.reshape(row_total, cache_size, head_count, HEAD)
    value_heads = cache_values.reshape(row_total, cache_size, head_count, HEAD)
    valid_mask = jnp.arange(cache_size)[None, :] < cache_lengths[:, None]
    own_keys = jnp.zeros((row_total, STEPS, local_width), jnp.bfloat16)
    hidden = hidden_rows.astype(jnp.float32)
    ssm_carry = ssm_state
    for step_index in range(STEPS):
        normed = (
            hidden * lax.rsqrt(jnp.mean(hidden * hidden, axis=1, keepdims=True) + norm_eps)
        ).astype(jnp.bfloat16)
        query_vals = project_query(normed)
        query_bf = query_vals.astype(jnp.bfloat16)
        own_keys = own_keys.at[:, step_index].set(query_bf)
        attended = attend(query_bf, key_heads, value_heads, valid_mask, own_keys, step_index)
        ssm_out, ssm_carry = ssm_update(query_vals, normed, ssm_carry, state_weight, decay_rate)
        mixed_out = (attended + ssm_out).astype(jnp.bfloat16)
        hidden = hidden + project_output(mixed_out)
    return hidden.astype(jnp.bfloat16)


def on_device(
    learner_input,
    cotangent,
    token_ids,
    rewards,
    group_ids,
    weight_master,
    adam_first,
    adam_second,
    hidden_rows,
    cache_keys,
    cache_values,
    cache_lengths,
    ssm_state,
    state_weight,
    decay_rate,
):
    local_tokens = token_ids.shape[0]
    local_seqs = local_tokens // SEQ
    advantage = group_advantage(rewards, group_ids)
    own_advantage = lax.dynamic_slice_in_dim(
        advantage, lax.axis_index("fsdp") * local_seqs, local_seqs, 0
    )
    token_adv = jnp.repeat(own_advantage, SEQ)
    token_weight = jnp.where(token_ids != 0, token_adv, 0.0) / SEQ
    signal = (token_weight[:, None] * cotangent.astype(jnp.float32)).astype(jnp.bfloat16)
    gradient = lax.psum_scatter(
        lax.dot_general(
            signal, learner_input, (((0,), (0,)), ((), ())), preferred_element_type=jnp.float32
        ),
        "fsdp",
        scatter_dimension=0,
        tiled=True,
    )
    new_first = beta_one * adam_first + (1.0 - beta_one) * gradient
    new_second = beta_two * adam_second + (1.0 - beta_two) * gradient * gradient
    update = (
        new_first
        / (1.0 - beta_one**adam_step)
        / (jnp.sqrt(new_second / (1.0 - beta_two**adam_step)) + adam_eps)
    )
    new_weight = weight_master - learn_rate * (update + weight_decay * weight_master)
    weight_bf = new_weight.astype(jnp.bfloat16)
    wide_rows = lax.all_gather(weight_bf, "grp", axis=1, tiled=True)
    head_block = lax.all_gather(wide_rows, "fsdp", axis=0, tiled=True)

    def project_query(normed):
        return lax.dot_general(
            normed, head_block, (((1,), (1,)), ((), ())), preferred_element_type=jnp.float32
        )

    def project_output(mixed_out):
        partial_sum = jnp.dot(mixed_out, head_block, preferred_element_type=jnp.float32)
        return lax.psum(partial_sum, "tp")

    decoded = decode_rows(
        hidden_rows,
        cache_keys,
        cache_values,
        cache_lengths,
        ssm_state,
        state_weight,
        decay_rate,
        project_query,
        project_output,
    )
    return (new_weight, new_first, new_second, decoded)


def solution(mesh):
    in_specs = (
        P("fsdp", "grp"),
        P("fsdp", "tp"),
        P("fsdp"),
        P(),
        P(),
        P(("tp", "fsdp"), "grp"),
        P(("tp", "fsdp"), "grp"),
        P(("tp", "fsdp"), "grp"),
        P(("fsdp", "grp"), None),
        P(("fsdp", "grp"), None, "tp"),
        P(("fsdp", "grp"), None, "tp"),
        P(("fsdp", "grp")),
        P(("fsdp", "grp"), None, "tp"),
        P(),
        P("tp"),
    )
    out_specs = (
        P(("tp", "fsdp"), "grp"),
        P(("tp", "fsdp"), "grp"),
        P(("tp", "fsdp"), "grp"),
        P(("fsdp", "grp"), None),
    )
    return jax.shard_map(
        on_device, mesh=mesh, in_specs=in_specs, out_specs=out_specs, check_vma=False
    )
```

profile of v0, /device:TPU:1, one launch (start us, length us, event | category | flops | bytes accessed | tf_op | source)
XLA Modules:
  0.0 460.9 jit_solution(8554968772199926769)
XLA Ops:
  7.2 1.0 fusion.25
  8.2 0.7 divide_subtract_fusion
  9.1 0.7 select_multiply_fusion
  9.8 8.2 %fusion = f32[1280,1280]{1,0:T(8,128)} fusion(bf16[1024,1280]{1,0:T(8,128)(2,1)S(1)} %copy-done, bf16[1024,1280]{1,0:T(8,128)(2,1)} %param.24, f32[1024]{0:T(1024)S(1)} %select_multiply_fusion), kind=kOutput, calls=%fused_computation.1 | convolution fusion | flops 3359375360 | bytes 11800576 | tf_op jit(solution)/shard_map/dot_general | solution.py:138
  18.0 95.3 %reduce-scatter.2.cloned.1.call-done = f32[80,1280]{1,0:T(8,128)} async-done(((f32[1280,1280]{1,0:T(8,128)}), f32[80,1280]{1,0:T(8,128)}) %reduce-scatter.2.cloned.1.call-update) | async-done | bytes 409616 | tf_op jit(solution)/shard_map/reduce_scatter | solution.py:137
  113.3 2.3 fusion.114
  115.7 11.6 %all_gather.6 = bf16[80,5120]{1,0:T(8,128)(2,1)} all-gather(bf16[80,1280]{1,0:T(8,128)(2,1)S(1)} %get-tuple-element.72), channel_id=1, replica_groups=mesh['fsdp'=16,'grp'=4,'tp'=4] {'grp'}, dimensions={1}, use_global_device_ids=true | all-gather | bytes 1024000 | tf_op jit(solution)/shard_map/all_gather | solution.py:154
  127.4 1.1 copy.47
  128.5 1.4 copy.53
  130.0 0.2 fusion.22
  130.2 2.2 fusion.99
  132.5 153.1 %all-gather.2.cloned.1.call-done = bf16[1280,5120]{1,0:T(8,128)(2,1)} async-done(((bf16[80,5120]{1,0:T(8,128)(2,1)}), bf16[1280,5120]{1,0:T(8,128)(2,1)}) %all-gather.2.cloned.1.call-update) | async-done | bytes 13107216 | tf_op jit(solution)/shard_map/all_gather | solution.py:155
  285.6 8.2 %multiply_exponential_fusion.3 = (f32[2,1280]{1,0:T(2,128)S(1)}, f32[2,1280]{1,0:T(2,128)S(1)}, bf16[2,1280]{1,0:T(2,128)(2,1)S(1)}) fusion(f32[1280]{0:T(1024)S(1)} %neg.20, bf16[1280,5120]{1,0:T(8,128)(2,1)} %all-gather.2.cloned.1.call-done, bf16[2,5120]{1,0:T(2,128)(2,1)S(1)} %copy-done.1, f32[2]{0:T(128)S(1)} %add_rsqrt_fusion.3), kind=kOutput, calls=%fused_computation.87 | convolution fusion | flops 26268160 | bytes 13158408 | tf_op jit(solution)/shard_map/dot_general | solution.py:158
  293.8 1.4 fusion.120
  296.0 0.2 fusion.113
  296.5 0.1 fusion.58
  296.8 0.4 fusion.44
  297.2 2.2 fusion.6
  299.5 6.5 %fusion.62 = f32[2,5120]{1,0:T(2,128)S(1)} fusion(bf16[1280,5120]{1,0:T(8,128)(2,1)} %all-gather.2.cloned.1.call-done, f32[1,2,10,128]{3,2,1,0:T(8,128)S(1)} %fusion.29, f32[2,1,1280]{2,1,0:T(1,128)S(1)} %fusion.6), kind=kOutput, calls=%fused_computation.109 | convolution fusion | flops 26219520 | bytes 13168640 | tf_op jit(solution)/shard_map/dot_general | solution.py:163
  306.0 18.7 %psum.28 = f32[2,5120]{1,0:T(2,128)S(1)} all-reduce(f32[2,5120]{1,0:T(2,128)S(1)} %fusion.62), channel_id=1, replica_groups=mesh['fsdp'=16,'grp'=4,'tp'=4] {'tp'}, use_global_device_ids=true, to_apply=%region_8.9 | all-reduce | flops 10240 | bytes 81920 | tf_op jit(solution)/shard_map/psum | solution.py:164
  324.7 0.2 multiply_reduce_fusion.2
  324.9 8.2 %bitcast_dynamic-update-slice_fusion.2 = (bf16[2,4,1280]{2,0,1:T(2,128)(2,1)S(1)}, bf16[2,1280]{1,0:T(2,128)(2,1)S(1)}, f32[2,1280]{1,0:T(2,128)S(1)}) fusion(bf16[2,4,1280]{2,0,1:T(2,128)(2,1)S(1)} %scatter.14, bf16[1280,5120]{1,0:T(8,128)(2,1)} %all-gather.2.cloned.1.call-done, f32[2]{0:T(128)S(1)} %add_rsqrt_fusion.2, f32[2,5120]{1,0:T(2,128)S(1)} %psum.28, ...), kind=kOutput, calls=%fused_computation.115 | convolution fusion | flops 26257920 | bytes 13189632 | tf_op jit(solution)/shard_map/dot_general | solution.py:158
  333.1 1.4 fusion.121
  335.2 0.2 fusion.112
  335.7 2.2 fusion.107
  338.3 0.4 fusion.42
  338.8 2.4 fusion.21
  341.1 6.5 %fusion.64 = f32[2,5120]{1,0:T(2,128)S(1)} fusion(bf16[1280,5120]{1,0:T(8,128)(2,1)} %all-gather.2.cloned.1.call-done, f32[1,2,10,128]{3,2,1,0:T(8,128)S(1)} %fusion.28, f32[2,1,1280]{2,1,0:T(1,128)S(1)} %fusion.21), kind=kOutput, calls=%fused_computation.110 | convolution fusion | flops 26219520 | bytes 13168640 | tf_op jit(solution)/shard_map/dot_general | solution.py:163
  347.7 20.8 %psum.29 = f32[2,5120]{1,0:T(2,128)S(1)} all-reduce(f32[2,5120]{1,0:T(2,128)S(1)} %fusion.64), channel_id=1, replica_groups=mesh['fsdp'=16,'grp'=4,'tp'=4] {'tp'}, use_global_device_ids=true, to_apply=%region_14.15 | all-reduce | flops 10240 | bytes 81920 | tf_op jit(solution)/shard_map/psum | solution.py:164
  368.4 0.2 multiply_reduce_fusion.1
  368.6 8.2 %bitcast_dynamic-update-slice_fusion.1 = (bf16[2,4,1280]{2,0,1:T(2,128)(2,1)S(1)}, bf16[2,1280]{1,0:T(2,128)(2,1)S(1)}, f32[2,1280]{1,0:T(2,128)S(1)}) fusion(bf16[2,4,1280]{2,0,1:T(2,128)(2,1)S(1)} %get-tuple-element.68, bf16[1280,5120]{1,0:T(8,128)(2,1)} %all-gather.2.cloned.1.call-done, f32[2,5120]{1,0:T(2,128)S(1)} %get-tuple-element.65, ...), kind=kOutput, calls=%fused_computation.114 | convolution fusion | flops 26237440 | bytes 13169152 | tf_op jit(solution)/shard_map/dot_general | solution.py:158
  376.9 1.4 fusion.122
  379.0 0.2 fusion.110
  379.4 2.2 fusion.103
  382.0 0.4 fusion.40
  382.5 2.5 fusion.7
  385.0 6.5 %fusion.66 = f32[2,5120]{1,0:T(2,128)S(1)} fusion(bf16[1280,5120]{1,0:T(8,128)(2,1)} %all-gather.2.cloned.1.call-done, f32[1,2,10,128]{3,2,1,0:T(8,128)S(1)} %fusion.27, f32[2,1,1280]{2,1,0:T(1,128)S(1)} %fusion.7), kind=kOutput, calls=%fused_computation.111 | convolution fusion | flops 26219520 | bytes 13168640 | tf_op jit(solution)/shard_map/dot_general | solution.py:163
  391.6 18.4 %psum.30 = f32[2,5120]{1,0:T(2,128)S(1)} all-reduce(f32[2,5120]{1,0:T(2,128)S(1)} %fusion.66), channel_id=1, replica_groups=mesh['fsdp'=16,'grp'=4,'tp'=4] {'tp'}, use_global_device_ids=true, to_apply=%region_20.21 | all-reduce | flops 10240 | bytes 81920 | tf_op jit(solution)/shard_map/psum | solution.py:164
  410.0 0.2 multiply_reduce_fusion
  410.2 8.2 %bitcast_dynamic-update-slice_fusion = (bf16[2,4,1280]{2,0,1:T(2,128)(2,1)S(1)}, bf16[2,1280]{1,0:T(2,128)(2,1)S(1)}, f32[2,1280]{1,0:T(2,128)S(1)}) fusion(bf16[2,4,1280]{2,0,1:T(2,128)(2,1)S(1)} %get-tuple-element.62, bf16[1280,5120]{1,0:T(8,128)(2,1)} %all-gather.2.cloned.1.call-done, f32[2,5120]{1,0:T(2,128)S(1)} %get-tuple-element.59, ...), kind=kOutput, calls=%fused_computation.113 | convolution fusion | flops 26237440 | bytes 13169152 | tf_op jit(solution)/shard_map/dot_general | solution.py:158
  418.4 1.4 fusion.123
  420.5 0.2 fusion.109
  421.0 2.2 fusion.105
  423.6 0.4 fusion.38
  424.1 2.6 fusion.2
  426.7 6.5 %fusion.68 = f32[2,5120]{1,0:T(2,128)S(1)} fusion(bf16[1280,5120]{1,0:T(8,128)(2,1)} %all-gather.2.cloned.1.call-done, f32[1,2,10,128]{3,2,1,0:T(8,128)S(1)} %fusion.26, f32[2,1,1280]{2,1,0:T(1,128)S(1)} %fusion.2), kind=kOutput, calls=%fused_computation.112 | convolution fusion | flops 26219520 | bytes 13168640 | tf_op jit(solution)/shard_map/dot_general | solution.py:163
  433.3 20.2 %psum.31 = f32[2,5120]{1,0:T(2,128)S(1)} all-reduce(f32[2,5120]{1,0:T(2,128)S(1)} %fusion.68), channel_id=1, replica_groups=mesh['fsdp'=16,'grp'=4,'tp'=4] {'tp'}, use_global_device_ids=true, to_apply=%region_26.27 | all-reduce | flops 10240 | bytes 81920 | tf_op jit(solution)/shard_map/psum | solution.py:164
  453.4 0.6 add_convert_fusion
  (110 shorter events, 6.1 us)
Async XLA Ops:
  7.2 2.6 copy-start
  7.2 106.2 %reduce-scatter.2.cloned.1.call-start = ((), (), s32[]{:S(2)}) async-start(), calls=%async_computation.1 | async-start | bytes 6963200 | tf_op jit(solution)/shard_map/reduce_scatter | solution.py:137
  17.9 95.4 %copy-start.3 = (f32[80,1280]{1,0:T(8,128)S(1)}, f32[80,1280]{1,0:T(8,128)}, u32[]{:S(2)}) copy-start(f32[80,1280]{1,0:T(8,128)} %param.28) | copy-start | bytes 1228804
  17.9 95.4 %copy-start.4 = (f32[80,1280]{1,0:T(8,128)S(1)}, f32[80,1280]{1,0:T(8,128)}, u32[]{:S(2)}) copy-start(f32[80,1280]{1,0:T(8,128)} %param.29) | copy-start | bytes 1228804
  18.0 267.6 %all-gather.2.cloned.1.call-start = ((), (), s32[]{:S(2)}) async-start(), calls=%async_computation.2 | async-start | bytes 13926400 | tf_op jit(solution)/shard_map/all_gather | solution.py:155
  115.7 11.7 %copy-start.5 = (f32[1280]{0:T(1024)S(1)}, f32[1280]{0:T(1024)}, u32[]{:S(2)}) copy-start(f32[1280]{0:T(1024)} %param.37) | copy-start | bytes 15364
  115.7 11.7 %copy-start.2 = (bf16[2,128,1280]{2,1,0:T(8,128)(2,1)S(1)}, bf16[2,128,1280]{2,1,0:T(8,128)(2,1)}, u32[]{:S(2)}) copy-start(bf16[2,128,1280]{2,1,0:T(8,128)(2,1)} %param.32) | copy-start | bytes 1966084
  127.4 2.6 copy-start.1
  127.4 2.7 copy-start.6
Sparse Core Ops, SparseCore 0:
  18.1 95.1 reduce-scatter.1
  127.5 158.0 all-gather.1
where the time goes:
time: 462 us; the launch traced here: 461 us
  waiting for transfers between devices  248 us (54%)
  matrix products  94.1 us (20%)
  blocking collectives  89.7 us (19%)
  between operations  14.4 us (3%)
  other arithmetic  8.9 us (2%)
  local copies, waits for them, and re-layouts  5.29 us (1%)
    all_gather x1, waiting for transfers between devices, on_device(): head_block = lax.all_gather(wide_rows, 'fsdp', axis=0, tiled=True)  153 us
    reduce_scatter x1, waiting for transfers between devices, on_device(): lax.psum_scatter(lax.dot_general(signal, learner_input, (((0,), (0,)), ((...  95.3 us
    psum x4, blocking collectives, project_output(): return lax.psum(partial_sum, 'tp')  78.1 us
    dot_general x4, matrix products, project_query(): lax.dot_general(normed, head_block, (((1,), (1,)), ((), ())), preferred_e...  32.8 us
    dot_general x4, matrix products, project_output(): jnp.dot(mixed_out, head_block, preferred_element_type=jnp.float32)  26.1 us
    all_gather x1, blocking collectives, on_device(): wide_rows = lax.all_gather(weight_bf, 'grp', axis=1, tiled=True)  11.6 us
    dot_general x4, matrix products, ssm_update(): jnp.einsum('rk,rkc->rc', out_gate, ssm_carry, precision=lax.Precision.HIG...  9.74 us
  transfers between devices with their start and end apart: 2, of which 2 were waited for; matrix products, arithmetic and copies ran while one was open for 1% of the time, Pallas kernels for 0%

commit v1 on v0

v1 whole, which is shorter than its diff:
```python
import functools
import math

import jax
import jax.numpy as jnp
from jax import lax
from jax.experimental import pallas as pl
from jax.experimental.pallas import tpu as pltpu
from jax.sharding import PartitionSpec as P

F32 = jnp.float32
BF16 = jnp.bfloat16
MESH = pl.DeviceIdType.MESH

D = 5120
HEAD = 128
NST = 128
SEQ = 256
STEPS = 4
BLK = 1280
SH = 80
TOK = 1024
CW = 256
CHUNKS = BLK // CW
HW = CW // 2
LC = 128
HEADS = BLK // HEAD
QW = BLK + 2 * NST + 128

beta_one = 0.9
beta_two = 0.95
learn_rate = 0.001
weight_decay = 0.1
adam_eps = 1e-08
adam_step = 10.0
norm_eps = 1e-05
mask_fill = -1e30

NT = (((1,), (1,)), ((), ()))


def kernel(
    inp_h, cot_h, ids_ref, rrow_ref, rcol_ref, grow_ref, gcol_ref,
    wm_h, m1_h, m2_h, hid_h, ck_h, cv_h, len_ref, st_h, sw_h, dec_ref,
    nw_h, nf_h, ns_h, out_ref,
    inp, cot, sigt, grad, wblk, ry, rz, zacc,
    wm, m1, m2, nw, nf, ns, hsrc, hbuf, ck, cv, st, sw,
    hid, own, qsend, qrecv, mixbuf, mix8, ps, c1r, c2s, c2r, tot, fbuf,
    lsem, ysend, yrecv, zsend, zrecv, azs, azr, ays, ayr,
    hs_s, hs_r, qs_s, qs_r, ms_s, ms_r, cs_s, cs_r, fs_s, fs_r,
):
    fs = lax.axis_index("fsdp")
    g = lax.axis_index("grp")
    tp = lax.axis_index("tp")
    z, y = fs // 4, fs % 4
    zhi, core = tp // 2, tp % 2

    def at_y(d):
        return {"fsdp": z * 4 + (y + d) % 4}

    def at_z(d):
        return {"fsdp": ((z + d) % 4) * 4 + y}

    def at_g(d):
        return {"grp": (g + d) % 4}

    mate = {"tp": zhi * 2 + (1 - core)}
    far = {"tp": (1 - zhi) * 2 + core}

    def send(src, dst, ssem, rsem, where):
        return pltpu.make_async_remote_copy(
            src_ref=src, dst_ref=dst, send_sem=ssem, recv_sem=rsem,
            device_id=where, device_id_type=MESH,
        )

    loads = [
        pltpu.make_async_copy(cot_h, cot, lsem.at[0]),
        pltpu.make_async_copy(inp_h, inp, lsem.at[1]),
        pltpu.make_async_copy(hid_h, hsrc, lsem.at[2]),
        pltpu.make_async_copy(wm_h, wm, lsem.at[3]),
        pltpu.make_async_copy(m1_h, m1, lsem.at[4]),
        pltpu.make_async_copy(m2_h, m2, lsem.at[5]),
        pltpu.make_async_copy(ck_h, ck, lsem.at[6]),
        pltpu.make_async_copy(cv_h, cv, lsem.at[7]),
        pltpu.make_async_copy(st_h, st, lsem.at[8]),
        pltpu.make_async_copy(
            sw_h.at[pl.ds(pl.multiple_of(g * BLK, BLK), BLK), :], sw, lsem.at[9]
        ),
    ]
    for copy in loads:
        copy.start()

    barrier = pltpu.get_barrier_semaphore()
    greeted = [at_y(1), at_y(3), at_z(1), at_z(3), at_g(1), at_g(2), at_g(3), mate, far]
    for where in greeted:
        pl.semaphore_signal(barrier, inc=1, device_id=where, device_id_type=MESH)

    same = (gcol_ref[...] == grow_ref[...]).astype(F32)
    adv = rrow_ref[...] - jnp.sum(same * rcol_ref[...], axis=0, keepdims=True) / jnp.sum(
        same, axis=0, keepdims=True
    )
    mine = lax.broadcasted_iota(jnp.int32, (8, 64), 1) == fs * 4 + (
        lax.broadcasted_iota(jnp.int32, (8, 64), 0) // 2
    )
    adv8 = jnp.sum(jnp.where(mine, jnp.broadcast_to(adv, (8, 64)), 0.0), axis=1, keepdims=True)
    tw = jnp.where(ids_ref[...] != 0, jnp.broadcast_to(adv8, (8, 128)), 0.0) / SEQ

    own[...] = jnp.zeros_like(own)

    loads[0].wait()

    def turn(j, _):
        col = pl.multiple_of(j * 128, 128)
        for k in range(TOK // 128):
            part = cot[k * 128 : (k + 1) * 128, pl.ds(col, 128)].T
            sigt[pl.ds(col, 128), k * 128 : (k + 1) * 128] = (
                part.astype(F32) * tw[k : k + 1, :]
            ).astype(BF16)
        return 0

    lax.fori_loop(0, BLK // 128, turn, 0)
    loads[1].wait()

    def gradient_chunk(c):
        def rows(q, _):
            part = jnp.dot(
                sigt[pl.ds(pl.multiple_of(q * 320, 320), 320), :],
                inp[:, c * CW : (c + 1) * CW],
                preferred_element_type=F32,
            )
            grad[q, :, :, c * CW : (c + 1) * CW] = part.astype(BF16).reshape(4, SH, CW)
            return 0

        lax.fori_loop(0, 4, rows, 0)

    wview = wblk.reshape(4, 4, SH, BLK)
    sent = []

    def go(copy):
        copy.start()
        sent.append(copy)
        return copy

    ylast, zlast, azlast, aylast = {}, {}, {}, {}

    def y_ring(c, s):
        for way, d in ((0, 1), (1, 3)):
            cols = pl.ds(c * CW + way * HW, HW)
            block = (y + 4 * (s + 1) - d * (s + 1)) % 4
            if s == 0:
                src = grad.at[:, block, :, cols]
            else:
                ylast[c, way].wait_recv()
                src = ry.at[c, s - 1, way]
                src[...] = (
                    src[...].astype(F32) + grad[:, block, :, c * CW + way * HW : c * CW + (way + 1) * HW].astype(F32)
                ).astype(BF16)
            ylast[c, way] = go(
                send(src, ry.at[c, s, way], ysend.at[c, s, way], yrecv.at[c, s, way], at_y(d))
            )

    def z_ring(c, s):
        block = (z + 3 - s) % 4
        if s == 0:
            for way in (0, 1):
                ylast[c, way].wait_recv()
                zacc[c, :, :, way * HW : (way + 1) * HW] = (
                    ry[c, 2, way].astype(F32)
                    + grad[:, y, :, c * CW + way * HW : c * CW + (way + 1) * HW].astype(F32)
                ).astype(BF16)
            src = zacc.at[c, block]
        else:
            zlast[c].wait_recv()
            src = rz.at[c, s - 1]
            src[...] = (src[...].astype(F32) + zacc[c, block].astype(F32)).astype(BF16)
        zlast[c] = go(send(src, rz.at[c, s], zsend.at[c, s], zrecv.at[c, s], at_z(1)))

    def adam(c):
        cols = slice(c * CW, (c + 1) * CW)
        zlast[c].wait_recv()
        grad_sum = rz[c, 2].astype(F32) + zacc[c, z].astype(F32)
        if c == 0:
            for copy in loads[3:6]:
                copy.wait()
        first = beta_one * m1[:, cols] + (1.0 - beta_one) * grad_sum
        second = beta_two * m2[:, cols] + (1.0 - beta_two) * grad_sum * grad_sum
        update = (
            first
            / (1.0 - beta_one**adam_step)
            / (jnp.sqrt(second / (1.0 - beta_two**adam_step)) + adam_eps)
        )
        master = wm[:, cols]
        fresh = master - learn_rate * (update + weight_decay * master)
        nf[:, cols] = first
        ns[:, cols] = second
        nw[:, cols] = fresh
        wblk[pl.ds(pl.multiple_of(fs * SH, 16), SH), cols] = fresh.astype(BF16)

    def z_gather(c, s):
        if s > 0:
            azlast[c].wait_recv()
        place = wview.at[(z + 4 - s) % 4, y, :, pl.ds(c * CW, CW)]
        azlast[c] = go(send(place, place, azs.at[c, s], azr.at[c, s], at_z(1)))

    def y_gather(c, s):
        if s == 0:
            azlast[c].wait_recv()
        for way, d in ((0, 1), (1, 3)):
            if s > 0:
                aylast[c, way].wait_recv()
            place = wview.at[:, (y + 4 * s - d * s) % 4, :, pl.ds(c * CW + way * HW, HW)]
            aylast[c, way] = go(
                send(place, place, ays.at[c, s, way], ayr.at[c, s, way], at_y(d))
            )

    def stage(c, s):
        if s < 3:
            y_ring(c, s)
        elif s < 6:
            z_ring(c, s - 3)
        elif s < 9:
            if s == 6:
                adam(c)
            z_gather(c, s - 6)
        elif s < 12:
            y_gather(c, s - 9)
        else:
            aylast[c, 0].wait_recv()
            aylast[c, 1].wait_recv()

    stores = [
        pltpu.make_async_copy(nw, nw_h, lsem.at[10]),
        pltpu.make_async_copy(nf, nf_h, lsem.at[11]),
        pltpu.make_async_copy(ns, ns_h, lsem.at[12]),
    ]
    for t in range(13 + CHUNKS - 1):
        if t < CHUNKS:
            gradient_chunk(t)
        if t == 0:
            loads[2].wait()
            pl.semaphore_wait(barrier, len(greeted))
        for c in range(CHUNKS):
            if 0 <= t - c < 13:
                stage(c, t - c)
        if t == 0:
            hcopies = [
                send(hsrc.at[(g + d) % 4], hbuf.at[g], hs_s.at[d - 1], hs_r.at[d - 1], at_g(d))
                for d in (1, 2, 3)
            ]
            for copy in hcopies:
                copy.start()
            hbuf[g] = hsrc[g]
        if t == 6 + CHUNKS - 1:
            for copy in stores:
                copy.start()

    for copy in hcopies:
        copy.wait()
    for i in range(4):
        hid[2 * i : 2 * i + 2, :] = hbuf[i]
    for copy in loads[6:]:
        copy.wait()

    head_of = (
        lax.broadcasted_iota(jnp.int32, (16, BLK), 1) // HEAD
        == lax.broadcasted_iota(jnp.int32, (16, BLK), 0)
    )
    own_row = lax.broadcasted_iota(jnp.int32, (16, BLK), 0)
    place128 = lax.broadcasted_iota(jnp.int32, (16, LC), 1)
    place16 = lax.broadcasted_iota(jnp.int32, (16, 16), 1)
    score_scale = 1.0 / math.sqrt(HEAD)

    def decode_step(s, _):
        h = hid[...]
        high = h.astype(BF16).astype(F32)
        both = jnp.concatenate([high, h - high], axis=0).astype(BF16)
        for n in range(CHUNKS):
            part = lax.dot_general(
                both, wblk[n * 256 : (n + 1) * 256, :], NT, preferred_element_type=F32
            )
            part = part[0:8] + part[8:16]
            for i in range(4):
                qsend[s, i, :, n * 256 : (n + 1) * 256] = part[2 * i : 2 * i + 2]
        part = jnp.dot(both, sw[...], preferred_element_type=F32)
        part = part[0:8] + part[8:16]
        square = jnp.broadcast_to(jnp.sum(h * h, axis=1, keepdims=True), (8, 128))
        for i in range(4):
            qsend[s, i, :, BLK : BLK + 2 * NST] = part[2 * i : 2 * i + 2]
            qsend[s, i, :, BLK + 2 * NST :] = square[2 * i : 2 * i + 2]
        copies = [
            send(
                qsend.at[s, (g + d) % 4], qrecv.at[s, d - 1],
                qs_s.at[s, d - 1], qs_r.at[s, d - 1], at_g(d),
            )
            for d in (1, 2, 3)
        ]
        for copy in copies:
            copy.start()
        total = qsend[s, g]
        for d, copy in enumerate(copies):
            copy.wait_recv()
            total = total + qrecv[s, d]
        scale = lax.rsqrt(total[:, BLK + 2 * NST : BLK + 2 * NST + 1] * (1.0 / D) + norm_eps)
        query = total[:, 0:BLK] * scale
        gates = total[:, BLK : BLK + 2 * NST] * scale
        query_bf = query.astype(BF16).astype(F32)
        step_size = jnp.maximum(query, 0.0) + jnp.log1p(jnp.exp(-jnp.abs(query)))
        decay = jnp.exp(-dec_ref[...] * step_size)
        drive = step_size * query

        for r in range(2):
            qrow = jnp.broadcast_to(query_bf[r : r + 1, :], (16, BLK))
            own_now = jnp.where(own_row == s, qrow, own[r])
            own[r] = own_now
            own_bf = own_now.astype(BF16)
            qhead = jnp.where(head_of, qrow, 0.0).astype(BF16)
            live = place128 < len_ref[r]
            mine_live = place16 <= s
            score = lax.dot_general(qhead, ck[r], NT, preferred_element_type=F32) * score_scale
            score_own = lax.dot_general(qhead, own_bf, NT, preferred_element_type=F32) * score_scale
            score = jnp.where(live, score, mask_fill)
            score_own = jnp.where(mine_live, score_own, mask_fill)
            top = jnp.maximum(
                jnp.max(score, axis=1, keepdims=True), jnp.max(score_own, axis=1, keepdims=True)
            )
            weight = jnp.where(live, jnp.exp(score - top), 0.0)
            weight_own = jnp.where(mine_live, jnp.exp(score_own - top), 0.0)
            norm = jnp.sum(weight, axis=1, keepdims=True) + jnp.sum(
                weight_own, axis=1, keepdims=True
            )
            prob = (weight / norm).astype(BF16)
            prob_own = (weight_own / norm).astype(BF16)
            attended = jnp.dot(prob, cv[r], preferred_element_type=F32) + jnp.dot(
                prob_own, own_bf, preferred_element_type=F32
            )
            attended = jnp.sum(jnp.where(head_of, attended, 0.0), axis=0, keepdims=True)
            in_gate = jnp.broadcast_to(gates[r : r + 1, 0:NST], (NST, NST)).T
            out_gate = jnp.broadcast_to(gates[r : r + 1, NST:], (NST, NST)).T
            for j in range(HEADS):
                cols = slice(j * 128, (j + 1) * 128)
                now = decay[r : r + 1, cols] * st[r, :, cols] + in_gate * drive[r : r + 1, cols]
                st[r, :, cols] = now
                mixed = attended[:, cols] + jnp.sum(out_gate * now, axis=0, keepdims=True)
                mixbuf[s, g, r : r + 1, cols] = mixed.astype(BF16).astype(F32)

        copies2 = [
            send(
                mixbuf.at[s, g], mixbuf.at[s, g],
                ms_s.at[s, d - 1], ms_r.at[s, d - 1], at_g(d),
            )
            for d in (1, 2, 3)
        ]
        for copy in copies2:
            copy.start()
        for copy in copies2:
            copy.wait_recv()
        for i in range(4):
            mix8[2 * i : 2 * i + 2, :] = mixbuf[s, i]
        lhs = mix8[...].astype(BF16)

        def half(which):
            cols = pl.ds(pl.multiple_of(which * 640, 128), 640)
            return jnp.dot(lhs, wblk[:, cols], preferred_element_type=F32)

        ps[s] = half(1 - core)
        one = send(ps.at[s], c1r.at[s], cs_s.at[s, 0], cs_r.at[s, 0], mate)
        one.start()
        mine_half = half(core)
        one.wait_recv()
        c2s[s] = mine_half + c1r[s]
        two = send(c2s.at[s], c2r.at[s], cs_s.at[s, 1], cs_r.at[s, 1], far)
        two.start()
        two.wait_recv()
        tot[s, core] = c2s[s] + c2r[s]
        three = send(tot.at[s, core], tot.at[s, core], cs_s.at[s, 2], cs_r.at[s, 2], mate)
        three.start()
        three.wait_recv()
        hid[:, 0:640] = hid[:, 0:640] + tot[s, 0]
        hid[:, 640:] = hid[:, 640:] + tot[s, 1]
        for copy in copies + copies2 + [one, two, three]:
            copy.wait_send()
        return 0

    lax.fori_loop(0, STEPS, decode_step, 0)

    for i in range(4):
        hsrc[i] = hid[2 * i : 2 * i + 2, :]
    last = [
        go(send(hsrc.at[(g + d) % 4], fbuf.at[g], fs_s.at[d - 1], fs_r.at[d - 1], at_g(d)))
        for d in (1, 2, 3)
    ]
    fbuf[g] = hsrc[g]
    for copy in last:
        copy.wait_recv()
    for i in range(4):
        out_ref[:, i * BLK : (i + 1) * BLK] = fbuf[i].astype(BF16)
    for copy in stores:
        copy.wait()
    for copy in sent:
        copy.wait_send()


def on_device(
    learner_input, cotangent, token_ids, rewards, group_ids, weight_master, adam_first,
    adam_second, hidden_rows, cache_keys, cache_values, cache_lengths, ssm_state,
    state_weight, decay_rate,
):
    hidden = hidden_rows.astype(F32).reshape(2, 4, BLK).transpose(1, 0, 2)
    hbm = pl.BlockSpec(memory_space=pl.ANY)
    vmem = pl.BlockSpec(memory_space=pltpu.VMEM)
    smem = pl.BlockSpec(memory_space=pltpu.SMEM)
    dma = pltpu.SemaphoreType.DMA
    V = pltpu.VMEM
    shard = jax.ShapeDtypeStruct((SH, BLK), F32)
    return pl.pallas_call(
        kernel,
        out_shape=(shard, shard, shard, jax.ShapeDtypeStruct((2, D), BF16)),
        in_specs=[hbm, hbm] + [vmem] * 5 + [hbm] * 6 + [smem] + [hbm] * 2 + [vmem],
        out_specs=(hbm, hbm, hbm, vmem),
        scratch_shapes=[
            V((TOK, BLK), BF16), V((TOK, BLK), BF16), V((BLK, TOK), BF16),
            V((4, 4, SH, BLK), BF16), V((BLK, BLK), BF16),
            V((CHUNKS, 3, 2, 4, SH, HW), BF16), V((CHUNKS, 3, SH, CW), BF16),
            V((CHUNKS, 4, SH, CW), BF16),
            V((SH, BLK), F32), V((SH, BLK), F32), V((SH, BLK), F32),
            V((SH, BLK), F32), V((SH, BLK), F32), V((SH, BLK), F32),
            V((4, 2, BLK), F32), V((4, 2, BLK), F32),
            V((2, LC, BLK), BF16), V((2, LC, BLK), BF16), V((2, NST, BLK), F32),
            V((BLK, 2 * NST), BF16),
            V((8, BLK), F32), V((2, 16, BLK), F32),
            V((STEPS, 4, 2, QW), F32), V((STEPS, 3, 2, QW), F32),
            V((STEPS, 4, 2, BLK), F32), V((8, BLK), F32),
            V((STEPS, 8, 640), F32), V((STEPS, 8, 640), F32), V((STEPS, 8, 640), F32),
            V((STEPS, 8, 640), F32), V((STEPS, 2, 8, 640), F32), V((4, 2, BLK), F32),
            dma((13,)),
            dma((CHUNKS, 3, 2)), dma((CHUNKS, 3, 2)), dma((CHUNKS, 3)), dma((CHUNKS, 3)),
            dma((CHUNKS, 3)), dma((CHUNKS, 3)), dma((CHUNKS, 3, 2)), dma((CHUNKS, 3, 2)),
            dma((3,)), dma((3,)), dma((STEPS, 3)), dma((STEPS, 3)),
            dma((STEPS, 3)), dma((STEPS, 3)), dma((STEPS, 3)), dma((STEPS, 3)),
            dma((3,)), dma((3,)),
        ],
        compiler_params=pltpu.CompilerParams(
            collective_id=0, has_side_effects=True, vmem_limit_bytes=56 * 1024 * 1024
        ),
    )(
        learner_input, cotangent, token_ids.reshape(8, 128),
        rewards.reshape(1, 64), rewards.reshape(64, 1),
        group_ids.reshape(1, 64), group_ids.reshape(64, 1),
        weight_master, adam_first, adam_second, hidden, cache_keys, cache_values,
        cache_lengths, ssm_state, state_weight, decay_rate.reshape(1, BLK),
    )


def solution(mesh):
    in_specs = (
        P("fsdp", "grp"), P("fsdp", "tp"), P("fsdp"), P(), P(),
        P(("tp", "fsdp"), "grp"), P(("tp", "fsdp"), "grp"), P(("tp", "fsdp"), "grp"),
        P(("fsdp", "grp"), None), P(("fsdp", "grp"), None, "tp"),
        P(("fsdp", "grp"), None, "tp"), P(("fsdp", "grp")),
        P(("fsdp", "grp"), None, "tp"), P(), P("tp"),
    )
    out_specs = (
        P(("tp", "fsdp"), "grp"), P(("tp", "fsdp"), "grp"), P(("tp", "fsdp"), "grp"),
        P(("fsdp", "grp"), None),
    )
    return jax.shard_map(
        on_device, mesh=mesh, in_specs=in_specs, out_specs=out_specs, check_vma=False
    )
```

time: 462 us -> 170 us (0.37)
  waiting for transfers between devices: 248 us -> 0 us
  Pallas kernels: 0 us -> 157 us
  matrix products: 94.1 us -> 0 us
  blocking collectives: 89.7 us -> 0 us
  between operations: 14.4 us -> 0.64 us
  other arithmetic: 8.9 us -> 1.36 us
  local copies, waits for them, and re-layouts: 5.29 us -> 10.7 us
    pallas_call x0 -> x1, Pallas kernels: none -> 157 us  [on_device(): pl.pallas_call(kernel, out_shape=(shard, shard, shard, jax.ShapeDtypeStru...]
    all_gather x1 -> x0, waiting for transfers between devices: 153 us -> none  [on_device(): head_block = lax.all_gather(wide_rows, 'fsdp', axis=0, tiled=True)]
    reduce_scatter x1 -> x0, waiting for transfers between devices: 95.3 us -> none  [on_device(): lax.psum_scatter(lax.dot_general(signal, learner_input, (((0,), (0,)), ((...]
    dot_general x33 -> x0, matrix products: 94.1 us -> none  [the longest x4 32.8 us: project_query(): lax.dot_general(normed, head_block, (((1,), (1,)), ((), ())), preferred_e...]
    psum x4 -> x0, blocking collectives: 78.1 us -> none  [project_output(): return lax.psum(partial_sum, 'tp')]
    all_gather x1 -> x0, blocking collectives: 11.6 us -> none  [on_device(): wide_rows = lax.all_gather(weight_bf, 'grp', axis=1, tiled=True)]
  transfers between devices with their start and end apart: 2 -> 0, of which waited for: 2 -> 0; matrix products, arithmetic and copies ran while one was open for 1% -> 0% of each run, Pallas kernels for 0% -> 0%
where the time goes in v1:
time: 170 us; the launch traced here: 169 us
  Pallas kernels  157 us (92%)
  local copies, waits for them, and re-layouts  10.7 us (6%)
    pallas_call x1, Pallas kernels, on_device(): pl.pallas_call(kernel, out_shape=(shard, shard, shard, jax.ShapeDtypeStru...  157 us
    unnamed x4, local copies, waits for them, and re-layouts  6.68 us

profile of v1, /device:TPU:1, one launch (start us, length us, event | category | flops | bytes accessed | tf_op | source)
XLA Modules:
  0.0 169.5 jit_solution(1161536487591892838)
XLA Ops:
  0.6 1.3 reshape.36.dec_ref
  1.9 1.4 copy.20.gcol_ref
  3.3 1.4 copy.19.rcol_ref
  4.6 1.4 convert_bitcast_fusion.hid_h
  6.0 156.8 %shard_map.174 = (f32[80,1280]{1,0:T(8,128)}, f32[80,1280]{1,0:T(8,128)}, f32[80,1280]{1,0:T(8,128)}, bf16[2,5120]{1,0:T(2,128)(2,1)}) custom-call(bf16[1024,1280]{1,0:T(8,128)(2,1)} %inp_h.1, bf16[1024,1280]{1,0:T(8,128)(2,1)} %cot_h.1, s32[8,128]{1,0:T(8,128)} %bitcast.10, f32[1,64]{1,0:T(1,128)} %bitcast.12, f32[64,1]{1,0:T(8,128)} %copy.19.rcol_ref, ...), custom_call_target="tpu_custom_call" | custom-call | tf_op jit(solution)/shard_map/pallas_call | solution.py:415
  162.8 1.8 %copy.25 = f32[80,1280]{1,0:T(8,128)} copy(f32[80,1280]{1,0:T(8,128)} %get-tuple-element.8) | data formatting | bytes 819200
  164.6 1.8 %copy.26 = f32[80,1280]{1,0:T(8,128)} copy(f32[80,1280]{1,0:T(8,128)} %get-tuple-element.9) | data formatting | bytes 819200
  166.4 1.8 %copy.27 = f32[80,1280]{1,0:T(8,128)} copy(f32[80,1280]{1,0:T(8,128)} %get-tuple-element.10) | data formatting | bytes 819200
  168.1 1.3 copy.28

commit v2 on v1

v2 whole, which is shorter than its diff:
```python
import functools
import math

import jax
import jax.numpy as jnp
from jax import lax
from jax.experimental import pallas as pl
from jax.experimental.pallas import tpu as pltpu
from jax.sharding import PartitionSpec as P

F32 = jnp.float32
BF16 = jnp.bfloat16
MESH = pl.DeviceIdType.MESH

D = 5120
HEAD = 128
NST = 128
SEQ = 256
STEPS = 4
BLK = 1280
SH = 80
TOK = 1024
CW = 256
CHUNKS = BLK // CW
HW = CW // 2
LC = 128
HEADS = BLK // HEAD
QW = BLK + 2 * NST + 128

beta_one = 0.9
beta_two = 0.95
learn_rate = 0.001
weight_decay = 0.1
adam_eps = 1e-08
adam_step = 10.0
norm_eps = 1e-05
mask_fill = -1e30

NT = (((1,), (1,)), ((), ()))


def adam_update(grad, master, first, second):
    first = beta_one * first + (1.0 - beta_one) * grad
    second = beta_two * second + (1.0 - beta_two) * grad * grad
    update = (
        first
        / (1.0 - beta_one**adam_step)
        / (jnp.sqrt(second / (1.0 - beta_two**adam_step)) + adam_eps)
    )
    return master - learn_rate * (update + weight_decay * master), first, second


def finish(grad, master, first, second, rows, nw, nf, ns, out):
    nw[...], nf[...], ns[...] = adam_update(grad[...], master[...], first[...], second[...])
    out[...] = rows[...]


def kernel(
    inp_h, cot_h, ids_ref, rew_ref, grp_ref,
    wm_h, m1_h, m2_h, hid_ref, ck_h, cv_h, len_ref, st_h, sw_h, dec_ref,
    gout_h, out_ref,
    inp, cot, sigt, grad, wblk, ry, rz, zacc,
    wm, m1, m2, gsum, hsrc, hbuf, ck, cv, st, sw, dec,
    hid, own, qsend, qrecv, mixbuf, mix8, cbuf, fsrc, fbuf,
    lsem, ysend, yrecv, zsend, zrecv, azs, azr, ays, ayr,
    hs_s, hs_r, qs_s, qs_r, ms_s, ms_r, cs_s, cs_r, fs_s, fs_r,
):
    fs = lax.axis_index("fsdp")
    g = lax.axis_index("grp")
    tp = lax.axis_index("tp")
    z, y = fs // 4, fs % 4

    def at_y(d):
        return {"fsdp": z * 4 + (y + d) % 4}

    def at_z(d):
        return {"fsdp": ((z + d) % 4) * 4 + y}

    def at_g(d):
        return {"grp": (g + d) % 4}

    def at_tp(d):
        return {"tp": (tp + d) % 4}

    def send(src, dst, ssem, rsem, where):
        return pltpu.make_async_remote_copy(
            src_ref=src, dst_ref=dst, send_sem=ssem, recv_sem=rsem,
            device_id=where, device_id_type=MESH,
        )

    loads = [
        pltpu.make_async_copy(cot_h, cot, lsem.at[0]),
        pltpu.make_async_copy(inp_h, inp, lsem.at[1]),
        pltpu.make_async_copy(wm_h, wm, lsem.at[2]),
        pltpu.make_async_copy(m1_h, m1, lsem.at[3]),
        pltpu.make_async_copy(m2_h, m2, lsem.at[4]),
        pltpu.make_async_copy(ck_h, ck, lsem.at[5]),
        pltpu.make_async_copy(cv_h, cv, lsem.at[6]),
        pltpu.make_async_copy(st_h, st, lsem.at[7]),
        pltpu.make_async_copy(
            sw_h.at[pl.ds(pl.multiple_of(g * BLK, BLK), BLK), :], sw, lsem.at[8]
        ),
    ]
    for copy in loads[:2]:
        copy.start()

    barrier = pltpu.get_barrier_semaphore()
    greeted = [at_y(1), at_y(3)] + [at(d) for at in (at_z, at_g, at_tp) for d in (1, 2, 3)]
    for where in greeted:
        pl.semaphore_signal(barrier, inc=1, device_id=where, device_id_type=MESH)

    diag = lax.broadcasted_iota(jnp.int32, (64, 64), 0) == lax.broadcasted_iota(
        jnp.int32, (64, 64), 1
    )
    ids_row = jnp.broadcast_to(grp_ref[...].astype(F32), (64, 64))
    rew_row = jnp.broadcast_to(rew_ref[...], (64, 64))
    ids_col = jnp.sum(jnp.where(diag, ids_row, 0.0), axis=1, keepdims=True)
    rew_col = jnp.sum(jnp.where(diag, rew_row, 0.0), axis=1, keepdims=True)
    same = (ids_row == ids_col).astype(F32)
    adv = rew_ref[...] - jnp.sum(same * rew_col, axis=0, keepdims=True) / jnp.sum(
        same, axis=0, keepdims=True
    )
    mine = lax.broadcasted_iota(jnp.int32, (8, 64), 1) == fs * 4 + (
        lax.broadcasted_iota(jnp.int32, (8, 64), 0) // 2
    )
    adv8 = jnp.sum(jnp.where(mine, jnp.broadcast_to(adv, (8, 64)), 0.0), axis=1, keepdims=True)
    tw = jnp.where(ids_ref[...] != 0, jnp.broadcast_to(adv8, (8, 128)), 0.0) / SEQ

    for i in range(4):
        hsrc[i] = hid_ref[:, i * BLK : (i + 1) * BLK].astype(F32)
    for j in range(HEADS):
        dec[0:1, j * 128 : (j + 1) * 128] = dec_ref[j : j + 1, :]
    own[...] = jnp.zeros_like(own)

    loads[0].wait()

    def turn(j, _):
        col = pl.multiple_of(j * 128, 128)
        for k in range(TOK // 128):
            part = cot[k * 128 : (k + 1) * 128, pl.ds(col, 128)].T
            sigt[pl.ds(col, 128), k * 128 : (k + 1) * 128] = (
                part.astype(F32) * tw[k : k + 1, :]
            ).astype(BF16)
        return 0

    lax.fori_loop(0, BLK // 128, turn, 0)
    loads[1].wait()
    for copy in loads[2:]:
        copy.start()

    def gradient_chunk(c):
        def rows(q, _):
            part = jnp.dot(
                sigt[pl.ds(pl.multiple_of(q * 320, 320), 320), :],
                inp[:, c * CW : (c + 1) * CW],
                preferred_element_type=F32,
            )
            grad[q, :, :, c * CW : (c + 1) * CW] = part.astype(BF16).reshape(4, SH, CW)
            return 0

        lax.fori_loop(0, 4, rows, 0)

    wview = wblk.reshape(4, 4, SH, BLK)
    sent = []

    def go(copy):
        copy.start()
        sent.append(copy)
        return copy

    F, B = 0, HW
    ylast, zlast, azlast, aylast = {}, {}, {}, {}

    def own_part(c, block, side):
        return grad[:, block, :, c * CW + side : c * CW + side + HW].astype(F32)

    def y_send(c, k, src, d):
        ylast[c, k] = go(send(src, ry.at[c, k], ysend.at[c, k], yrecv.at[c, k], at_y(d)))

    def reduce_a(c):
        for k, block, side, d in ((0, 2, F, 1), (2, 2, B, 3), (1, 1, B, 1), (3, 3, F, 3)):
            y_send(c, k, grad.at[:, (y + block) % 4, :, pl.ds(c * CW + side, HW)], d)

    def reduce_b(c):
        for k, block, side, d in ((0, 1, F, 1), (2, 3, B, 3)):
            ylast[c, k].wait_recv()
            ry[c, k] = (ry[c, k].astype(F32) + own_part(c, (y + block) % 4, side)).astype(BF16)
            y_send(c, 4 + k // 2, ry.at[c, k], d)

    def reduce_z(c):
        for k, last, side in ((3, 4, F), (1, 5, B)):
            ylast[c, k].wait_recv()
            ylast[c, last].wait_recv()
            zacc[c, :, :, side : side + HW] = (
                own_part(c, y, side) + ry[c, k].astype(F32) + ry[c, last].astype(F32)
            ).astype(BF16)
        for d in (1, 2, 3):
            zlast[c, d] = go(
                send(
                    zacc.at[c, (z + d) % 4], rz.at[c, d - 1],
                    zsend.at[c, d - 1], zrecv.at[c, d - 1], at_z(d),
                )
            )

    def adam(c):
        cols = slice(c * CW, (c + 1) * CW)
        total = zacc[c, z].astype(F32)
        for d in (1, 2, 3):
            zlast[c, d].wait_recv()
            total = total + rz[c, d - 1].astype(F32)
        if c == 0:
            for copy in loads[2:5]:
                copy.wait()
        gsum[:, cols] = total
        fresh = adam_update(total, wm[:, cols], m1[:, cols], m2[:, cols])[0]
        wblk[pl.ds(pl.multiple_of(fs * SH, 16), SH), cols] = fresh.astype(BF16)
        for d in (1, 2, 3):
            place = wview.at[z, y, :, pl.ds(c * CW, CW)]
            azlast[c, d] = go(send(place, place, azs.at[c, d - 1], azr.at[c, d - 1], at_z(d)))

    def gather_a(c):
        for d in (1, 2, 3):
            azlast[c, d].wait_recv()
        for k, d in ((0, 1), (1, 3)):
            place = wview.at[:, y, :, pl.ds(c * CW, CW)]
            aylast[c, k] = go(send(place, place, ays.at[c, k], ayr.at[c, k], at_y(d)))

    def gather_b(c):
        for k, block, side, d in ((0, 3, F, 1), (1, 1, B, 3)):
            aylast[c, k].wait_recv()
            place = wview.at[:, (y + block) % 4, :, pl.ds(c * CW + side, HW)]
            aylast[c, k + 2] = go(
                send(place, place, ays.at[c, k + 2], ayr.at[c, k + 2], at_y(d))
            )

    def gather_end(c):
        aylast[c, 2].wait_recv()
        aylast[c, 3].wait_recv()

    stages = (reduce_a, reduce_b, reduce_z, adam, gather_a, gather_b, gather_end)
    store = pltpu.make_async_copy(gsum, gout_h, lsem.at[9])
    hcopies = [
        send(hsrc.at[(g + d) % 4], hbuf.at[g], hs_s.at[d - 1], hs_r.at[d - 1], at_g(d))
        for d in (1, 2, 3)
    ]
    for t in range(len(stages) + CHUNKS - 1):
        if t < CHUNKS:
            gradient_chunk(t)
        if t == 0:
            pl.semaphore_wait(barrier, len(greeted))
        for c in range(CHUNKS):
            if 0 <= t - c < len(stages):
                stages[t - c](c)
        if t == 0:
            for copy in hcopies:
                copy.start()
            hbuf[g] = hsrc[g]
        if t == 3 + CHUNKS - 1:
            store.start()

    for copy in hcopies:
        copy.wait()
    for i in range(4):
        hid[2 * i : 2 * i + 2, :] = hbuf[i]
    for copy in loads[5:]:
        copy.wait()

    head_of = (
        lax.broadcasted_iota(jnp.int32, (16, BLK), 1) // HEAD
        == lax.broadcasted_iota(jnp.int32, (16, BLK), 0)
    )
    own_row = lax.broadcasted_iota(jnp.int32, (16, BLK), 0)
    place128 = lax.broadcasted_iota(jnp.int32, (16, LC), 1)
    place16 = lax.broadcasted_iota(jnp.int32, (16, 16), 1)
    score_scale = 1.0 / math.sqrt(HEAD)

    def decode_step(s, _):
        h = hid[...]
        high = h.astype(BF16).astype(F32)
        both = jnp.concatenate([high, h - high], axis=0).astype(BF16)
        for n in range(CHUNKS):
            part = lax.dot_general(
                both, wblk[n * 256 : (n + 1) * 256, :], NT, preferred_element_type=F32
            )
            part = part[0:8] + part[8:16]
            for i in range(4):
                qsend[s, i, :, n * 256 : (n + 1) * 256] = part[2 * i : 2 * i + 2]
        part = jnp.dot(both, sw[...], preferred_element_type=F32)
        part = part[0:8] + part[8:16]
        square = jnp.broadcast_to(jnp.sum(h * h, axis=1, keepdims=True), (8, 128))
        for i in range(4):
            qsend[s, i, :, BLK : BLK + 2 * NST] = part[2 * i : 2 * i + 2]
            qsend[s, i, :, BLK + 2 * NST :] = square[2 * i : 2 * i + 2]
        copies = [
            send(
                qsend.at[s, (g + d) % 4], qrecv.at[s, d - 1],
                qs_s.at[s, d - 1], qs_r.at[s, d - 1], at_g(d),
            )
            for d in (1, 2, 3)
        ]
        for copy in copies:
            copy.start()
        total = qsend[s, g]
        for d, copy in enumerate(copies):
            copy.wait_recv()
            total = total + qrecv[s, d]
        scale = lax.rsqrt(total[:, BLK + 2 * NST : BLK + 2 * NST + 1] * (1.0 / D) + norm_eps)
        query = total[:, 0:BLK] * scale
        gates = total[:, BLK : BLK + 2 * NST] * scale
        query_bf = query.astype(BF16).astype(F32)
        step_size = jnp.maximum(query, 0.0) + jnp.log1p(jnp.exp(-jnp.abs(query)))
        decay = jnp.exp(-dec[...] * step_size)
        drive = step_size * query

        in_gates = []
        for r in range(2):
            qrow = jnp.broadcast_to(query_bf[r : r + 1, :], (16, BLK))
            own_now = jnp.where(own_row == s, qrow, own[r])
            own[r] = own_now
            own_bf = own_now.astype(BF16)
            qhead = jnp.where(head_of, qrow, 0.0).astype(BF16)
            live = place128 < len_ref[r]
            mine_live = place16 <= s
            score = lax.dot_general(qhead, ck[r], NT, preferred_element_type=F32) * score_scale
            score_own = lax.dot_general(qhead, own_bf, NT, preferred_element_type=F32) * score_scale
            score = jnp.where(live, score, mask_fill)
            score_own = jnp.where(mine_live, score_own, mask_fill)
            top = jnp.maximum(
                jnp.max(score, axis=1, keepdims=True), jnp.max(score_own, axis=1, keepdims=True)
            )
            weight = jnp.where(live, jnp.exp(score - top), 0.0)
            weight_own = jnp.where(mine_live, jnp.exp(score_own - top), 0.0)
            norm = jnp.sum(weight, axis=1, keepdims=True) + jnp.sum(
                weight_own, axis=1, keepdims=True
            )
            prob = (weight / norm).astype(BF16)
            prob_own = (weight_own / norm).astype(BF16)
            attended = jnp.dot(prob, cv[r], preferred_element_type=F32) + jnp.dot(
                prob_own, own_bf, preferred_element_type=F32
            )
            attended = jnp.sum(jnp.where(head_of, attended, 0.0), axis=0, keepdims=True)
            in_row, out_row = gates[r : r + 1, 0:NST], gates[r : r + 1, NST:]
            out_gate = jnp.broadcast_to(out_row, (NST, NST)).T
            in_gates.append(in_row)
            both_gates = jnp.sum(in_row * out_row, axis=1, keepdims=True)
            for j in range(HEADS):
                cols = slice(j * 128, (j + 1) * 128)
                seen = jnp.sum(out_gate * st[r, :, cols], axis=0, keepdims=True)
                mixed = (
                    attended[:, cols]
                    + decay[r : r + 1, cols] * seen
                    + both_gates * drive[r : r + 1, cols]
                )
                mixbuf[s, g, r : r + 1, cols] = mixed.astype(BF16).astype(F32)

        copies2 = [
            send(
                mixbuf.at[s, g], mixbuf.at[s, g],
                ms_s.at[s, d - 1], ms_r.at[s, d - 1], at_g(d),
            )
            for d in (1, 2, 3)
        ]
        for copy in copies2:
            copy.start()
        for r in range(2):
            in_gate = jnp.broadcast_to(in_gates[r], (NST, NST)).T
            for j in range(HEADS):
                cols = slice(j * 128, (j + 1) * 128)
                st[r, :, cols] = (
                    decay[r : r + 1, cols] * st[r, :, cols] + in_gate * drive[r : r + 1, cols]
                )
        for copy in copies2:
            copy.wait_recv()
        for i in range(4):
            mix8[2 * i : 2 * i + 2, :] = mixbuf[s, i]
        lhs = mix8[...].astype(BF16)
        copies3 = []
        for half in range(2):
            cbuf[s, half, tp] = jnp.dot(
                lhs, wblk[:, half * 640 : (half + 1) * 640], preferred_element_type=F32
            )
            for d in (1, 2, 3):
                place = cbuf.at[s, half, tp]
                sems = cs_s.at[s, half, d - 1], cs_r.at[s, half, d - 1]
                copies3.append(send(place, place, *sems, at_tp(d)))
                copies3[-1].start()
        for half in range(2):
            for copy in copies3[3 * half : 3 * half + 3]:
                copy.wait_recv()
            cols = slice(half * 640, (half + 1) * 640)
            hid[:, cols] = hid[:, cols] + (
                (cbuf[s, half, 0] + cbuf[s, half, 1]) + (cbuf[s, half, 2] + cbuf[s, half, 3])
            )
        for copy in copies + copies2 + copies3:
            copy.wait_send()
        return 0

    lax.fori_loop(0, STEPS, decode_step, 0)

    for i in range(4):
        fsrc[i] = hid[2 * i : 2 * i + 2, :]
    last = [
        go(send(fsrc.at[(g + d) % 4], fbuf.at[g], fs_s.at[d - 1], fs_r.at[d - 1], at_g(d)))
        for d in (1, 2, 3)
    ]
    fbuf[g] = fsrc[g]
    for copy in last:
        copy.wait_recv()
    for i in range(4):
        out_ref[:, i * BLK : (i + 1) * BLK] = fbuf[i].astype(BF16)
    store.wait()
    for copy in sent:
        copy.wait_send()


def on_device(
    learner_input, cotangent, token_ids, rewards, group_ids, weight_master, adam_first,
    adam_second, hidden_rows, cache_keys, cache_values, cache_lengths, ssm_state,
    state_weight, decay_rate,
):
    hbm = pl.BlockSpec(memory_space=pl.ANY)
    vmem = pl.BlockSpec(memory_space=pltpu.VMEM)
    smem = pl.BlockSpec(memory_space=pltpu.SMEM)
    dma = pltpu.SemaphoreType.DMA
    V = pltpu.VMEM
    shard = jax.ShapeDtypeStruct((SH, BLK), F32)
    rows = jax.ShapeDtypeStruct((2, D), BF16)
    grad, decoded = pl.pallas_call(
        kernel,
        out_shape=(shard, rows),
        in_specs=[hbm, hbm] + [vmem] * 3 + [hbm] * 3 + [vmem] + [hbm] * 2 + [smem] + [hbm] * 2 + [vmem],
        out_specs=(hbm, vmem),
        scratch_shapes=[
            V((TOK, BLK), BF16), V((TOK, BLK), BF16), V((BLK, TOK), BF16),
            V((4, 4, SH, BLK), BF16), V((BLK, BLK), BF16),
            V((CHUNKS, 6, 4, SH, HW), BF16), V((CHUNKS, 3, SH, CW), BF16),
            V((CHUNKS, 4, SH, CW), BF16),
            V((SH, BLK), F32), V((SH, BLK), F32), V((SH, BLK), F32), V((SH, BLK), F32),
            V((4, 2, BLK), F32), V((4, 2, BLK), F32),
            V((2, LC, BLK), BF16), V((2, LC, BLK), BF16), V((2, NST, BLK), F32),
            V((BLK, 2 * NST), BF16), V((1, BLK), F32),
            V((8, BLK), F32), V((2, 16, BLK), F32),
            V((STEPS, 4, 2, QW), F32), V((STEPS, 3, 2, QW), F32),
            V((STEPS, 4, 2, BLK), F32), V((8, BLK), F32),
            V((STEPS, 2, 4, 8, 640), F32), V((4, 2, BLK), F32), V((4, 2, BLK), F32),
            dma((10,)),
            dma((CHUNKS, 6)), dma((CHUNKS, 6)), dma((CHUNKS, 3)), dma((CHUNKS, 3)),
            dma((CHUNKS, 3)), dma((CHUNKS, 3)), dma((CHUNKS, 4)), dma((CHUNKS, 4)),
            dma((3,)), dma((3,)), dma((STEPS, 3)), dma((STEPS, 3)),
            dma((STEPS, 3)), dma((STEPS, 3)), dma((STEPS, 2, 3)), dma((STEPS, 2, 3)),
            dma((3,)), dma((3,)),
        ],
        compiler_params=pltpu.CompilerParams(
            collective_id=0, has_side_effects=True, vmem_limit_bytes=56 * 1024 * 1024
        ),
    )(
        learner_input, cotangent, token_ids.reshape(8, 128), rewards.reshape(1, 64),
        group_ids.reshape(1, 64), weight_master, adam_first, adam_second, hidden_rows,
        cache_keys, cache_values, cache_lengths, ssm_state, state_weight,
        decay_rate.reshape(HEADS, 128),
    )
    part = pl.BlockSpec((SH, BLK // 2), lambda i: (0, i))
    whole = pl.BlockSpec((2, D), lambda i: (0, 0))
    return pl.pallas_call(
        finish,
        grid=(2,),
        out_shape=(shard, shard, shard, rows),
        in_specs=[part] * 4 + [whole],
        out_specs=(part, part, part, whole),
    )(grad, weight_master, adam_first, adam_second, decoded)


def solution(mesh):
    in_specs = (
        P("fsdp", "grp"), P("fsdp", "tp"), P("fsdp"), P(), P(),
        P(("tp", "fsdp"), "grp"), P(("tp", "fsdp"), "grp"), P(("tp", "fsdp"), "grp"),
        P(("fsdp", "grp"), None), P(("fsdp", "grp"), None, "tp"),
        P(("fsdp", "grp"), None, "tp"), P(("fsdp", "grp")),
        P(("fsdp", "grp"), None, "tp"), P(), P("tp"),
    )
    out_specs = (
        P(("tp", "fsdp"), "grp"), P(("tp", "fsdp"), "grp"), P(("tp", "fsdp"), "grp"),
        P(("fsdp", "grp"), None),
    )
    return jax.shard_map(
        on_device, mesh=mesh, in_specs=in_specs, out_specs=out_specs, check_vma=False
    )
```

time: 170 us -> 145 us (0.85)
  Pallas kernels: 157 us -> 144 us
  local copies, waits for them, and re-layouts: 10.7 us -> 0 us
    pallas_call x1 -> x2, Pallas kernels: 157 us -> 144 us  [the longest x1 141 us: on_device(): pl.pallas_call(kernel, out_shape=(shard, rows), in_specs=[hbm, hbm] + [vm...]
    unnamed x4 -> x0, local copies, waits for them, and re-layouts: 6.68 us -> none
    reshape x3 -> x0, local copies, waits for them, and re-layouts: 4.01 us -> none  [the longest x1 1.36 us: on_device(): group_ids.reshape(64, 1)]
where the time goes in v2:
time: 145 us; the launch traced here: 144 us
  Pallas kernels  144 us (99%)
    pallas_call x1, Pallas kernels, on_device(): pl.pallas_call(kernel, out_shape=(shard, rows), in_specs=[hbm, hbm] + [vm...  141 us

profile of v2, /device:TPU:1, one launch (start us, length us, event | category | flops | bytes accessed | tf_op | source)
XLA Modules:
  0.0 144.1 jit_solution(10550514375124134259)
XLA Ops:
  0.6 141.0 %shard_map.174 = (f32[80,1280]{1,0:T(8,128)}, bf16[2,5120]{1,0:T(2,128)(2,1)}) custom-call(bf16[1024,1280]{1,0:T(8,128)(2,1)} %inp_h.1, bf16[1024,1280]{1,0:T(8,128)(2,1)} %cot_h.1, s32[8,128]{1,0:T(8,128)} %bitcast.5, f32[1,64]{1,0:T(1,128)} %bitcast.6, s32[1,64]{1,0:T(1,128)} %bitcast.7, f32[80,1280]{1,0:T(8,128)} %master.1, f32[80,1280]{1,0:T(8,128)} %first.1, ...), custom_call_target="tpu_custom_call" | custom-call | tf_op jit(solution)/shard_map/pallas_call | solution.py:428
  141.7 2.5 %shard_map.175 = (f32[80,1280]{1,0:T(8,128)}, f32[80,1280]{1,0:T(8,128)}, f32[80,1280]{1,0:T(8,128)}, bf16[2,5120]{1,0:T(2,128)(2,1)}) custom-call(f32[80,1280]{1,0:T(8,128)} %get-tuple-element.6.grad, f32[80,1280]{1,0:T(8,128)} %master.1, f32[80,1280]{1,0:T(8,128)} %first.1, f32[80,1280]{1,0:T(8,128)} %second.1, bf16[2,5120]{1,0:T(2,128)(2,1)} %get-tuple-element.7.rows), custom_call_target="tpu_custom_call" | custom-call | tf_op jit(solution)/shard_map/pallas_call | solution.py:464

commit v3 on v2

--- a/solution.py
+++ b/solution.py
@@ -20,9 +20,9 @@
 BLK = 1280
 SH = 80
 TOK = 1024
-CW = 256
+CW = 128
 CHUNKS = BLK // CW
-HW = CW // 2
+LAG = (0, 2, 4, 6, 8, 10, 12)
 LC = 128
 HEADS = BLK // HEAD
 QW = BLK + 2 * NST + 128
@@ -78,6 +78,9 @@
 
     def at_g(d):
         return {"grp": (g + d) % 4}
+
+    def at_both(dg, dt):
+        return {"grp": (g + dg) % 4, "tp": (tp + dt) % 4}
 
     def at_tp(d):
         return {"tp": (tp + d) % 4}
@@ -106,6 +109,7 @@
 
     barrier = pltpu.get_barrier_semaphore()
     greeted = [at_y(1), at_y(3)] + [at(d) for at in (at_z, at_g, at_tp) for d in (1, 2, 3)]
+    greeted += [at_both(dg, dt) for dg in (1, 2, 3) for dt in (1, 2, 3)]
     for where in greeted:
         pl.semaphore_signal(barrier, inc=1, device_id=where, device_id_type=MESH)
 
@@ -152,10 +156,10 @@
         def rows(q, _):
             part = jnp.dot(
                 sigt[pl.ds(pl.multiple_of(q * 320, 320), 320), :],
-                inp[:, c * CW : (c + 1) * CW],
+                inp[:, c * 256 : (c + 1) * 256],
                 preferred_element_type=F32,
             )
-            grad[q, :, :, c * CW : (c + 1) * CW] = part.astype(BF16).reshape(4, SH, CW)
+            grad[q, :, :, c * 256 : (c + 1) * 256] = part.astype(BF16).reshape(4, SH, 256)
             return 0
 
         lax.fori_loop(0, 4, rows, 0)
@@ -168,18 +172,23 @@
         sent.append(copy)
         return copy
 
-    F, B = 0, HW
+    F, B = 0, 2
     ylast, zlast, azlast, aylast = {}, {}, {}, {}
 
+    def columns(c):
+        return pl.ds(c * CW, CW)
+
     def own_part(c, block, side):
-        return grad[:, block, :, c * CW + side : c * CW + side + HW].astype(F32)
+        return grad[side : side + 2, block, :, c * CW : (c + 1) * CW].astype(F32)
 
     def y_send(c, k, src, d):
         ylast[c, k] = go(send(src, ry.at[c, k], ysend.at[c, k], yrecv.at[c, k], at_y(d)))
 
     def reduce_a(c):
+        if c % 2 == 0 and c > 0:
+            gradient_chunk(c // 2)
         for k, block, side, d in ((0, 2, F, 1), (2, 2, B, 3), (1, 1, B, 1), (3, 3, F, 3)):
-            y_send(c, k, grad.at[:, (y + block) % 4, :, pl.ds(c * CW + side, HW)], d)
+            y_send(c, k, grad.at[pl.ds(side, 2), (y + block) % 4, :, columns(c)], d)
 
     def reduce_b(c):
         for k, block, side, d in ((0, 1, F, 1), (2, 3, B, 3)):
@@ -191,7 +200,7 @@
         for k, last, side in ((3, 4, F), (1, 5, B)):
             ylast[c, k].wait_recv()
             ylast[c, last].wait_recv()
-            zacc[c, :, :, side : side + HW] = (
+            zacc[c, side : side + 2] = (
                 own_part(c, y, side) + ry[c, k].astype(F32) + ry[c, last].astype(F32)
             ).astype(BF16)
         for d in (1, 2, 3):
@@ -202,33 +211,38 @@
                 )
             )
 
+    started = []
+
     def adam(c):
         cols = slice(c * CW, (c + 1) * CW)
         total = zacc[c, z].astype(F32)
         for d in (1, 2, 3):
             zlast[c, d].wait_recv()
             total = total + rz[c, d - 1].astype(F32)
-        if c == 0:
+        if not started:
             for copy in loads[2:5]:
                 copy.wait()
+        started.append(c)
         gsum[:, cols] = total
         fresh = adam_update(total, wm[:, cols], m1[:, cols], m2[:, cols])[0]
         wblk[pl.ds(pl.multiple_of(fs * SH, 16), SH), cols] = fresh.astype(BF16)
+        if len(started) == CHUNKS:
+            store.start()
+        place = wview.at[z, y, :, columns(c)]
         for d in (1, 2, 3):
-            place = wview.at[z, y, :, pl.ds(c * CW, CW)]
             azlast[c, d] = go(send(place, place, azs.at[c, d - 1], azr.at[c, d - 1], at_z(d)))
 
     def gather_a(c):
         for d in (1, 2, 3):
             azlast[c, d].wait_recv()
         for k, d in ((0, 1), (1, 3)):
-            place = wview.at[:, y, :, pl.ds(c * CW, CW)]
+            place = wview.at[:, y, :, columns(c)]
             aylast[c, k] = go(send(place, place, ays.at[c, k], ayr.at[c, k], at_y(d)))
 
     def gather_b(c):
         for k, block, side, d in ((0, 3, F, 1), (1, 1, B, 3)):
             aylast[c, k].wait_recv()
-            place = wview.at[:, (y + block) % 4, :, pl.ds(c * CW + side, HW)]
+            place = wview.at[pl.ds(side, 2), (y + block) % 4, :, columns(c)]
             aylast[c, k + 2] = go(
                 send(place, place, ays.at[c, k + 2], ayr.at[c, k + 2], at_y(d))
             )
@@ -243,20 +257,16 @@
         send(hsrc.at[(g + d) % 4], hbuf.at[g], hs_s.at[d - 1], hs_r.at[d - 1], at_g(d))
         for d in (1, 2, 3)
     ]
-    for t in range(len(stages) + CHUNKS - 1):
-        if t < CHUNKS:
-            gradient_chunk(t)
-        if t == 0:
-            pl.semaphore_wait(barrier, len(greeted))
-        for c in range(CHUNKS):
-            if 0 <= t - c < len(stages):
-                stages[t - c](c)
+    gradient_chunk(0)
+    pl.semaphore_wait(barrier, len(greeted))
+    for t in range(LAG[-1] + CHUNKS):
+        for stage, lag in zip(stages, LAG):
+            if 0 <= t - lag < CHUNKS:
+                stage(t - lag)
         if t == 0:
             for copy in hcopies:
                 copy.start()
             hbuf[g] = hsrc[g]
-        if t == 3 + CHUNKS - 1:
-            store.start()
 
     for copy in hcopies:
         copy.wait()
@@ -274,11 +284,19 @@
     place16 = lax.broadcasted_iota(jnp.int32, (16, 16), 1)
     score_scale = 1.0 / math.sqrt(HEAD)
 
-    def decode_step(s, _):
+    def tp_copies(s):
+        return [
+            send(
+                cbuf.at[s, tp], cbuf.at[s, tp], cs_s.at[s, d - 1], cs_r.at[s, d - 1], at_tp(d)
+            )
+            for d in (2, 1, 3)
+        ]
+
+    def decode_step(s, _, last=False):
         h = hid[...]
         high = h.astype(BF16).astype(F32)
         both = jnp.concatenate([high, h - high], axis=0).astype(BF16)
-        for n in range(CHUNKS):
+        for n in range(BLK // 256):
             part = lax.dot_general(
                 both, wblk[n * 256 : (n + 1) * 256, :], NT, preferred_element_type=F32
             )
@@ -362,7 +380,9 @@
         ]
         for copy in copies2:
             copy.start()
-        for r in range(2):
+        for copy in copies:
+            copy.wait_send()
+        for r in range(0 if last else 2):
             in_gate = jnp.broadcast_to(in_gates[r], (NST, NST)).T
             for j in range(HEADS):
                 cols = slice(j * 128, (j + 1) * 128)
@@ -374,43 +394,56 @@
         for i in range(4):
             mix8[2 * i : 2 * i + 2, :] = mixbuf[s, i]
         lhs = mix8[...].astype(BF16)
-        copies3 = []
-        for half in range(2):
-            cbuf[s, half, tp] = jnp.dot(
-                lhs, wblk[:, half * 640 : (half + 1) * 640], preferred_element_type=F32
-            )
-            for d in (1, 2, 3):
-                place = cbuf.at[s, half, tp]
-                sems = cs_s.at[s, half, d - 1], cs_r.at[s, half, d - 1]
-                copies3.append(send(place, place, *sems, at_tp(d)))
-                copies3[-1].start()
-        for half in range(2):
-            for copy in copies3[3 * half : 3 * half + 3]:
-                copy.wait_recv()
-            cols = slice(half * 640, (half + 1) * 640)
-            hid[:, cols] = hid[:, cols] + (
-                (cbuf[s, half, 0] + cbuf[s, half, 1]) + (cbuf[s, half, 2] + cbuf[s, half, 3])
-            )
-        for copy in copies + copies2 + copies3:
+        part = [
+            jnp.dot(lhs, wblk[:, half * 640 : (half + 1) * 640], preferred_element_type=F32)
+            for half in range(2)
+        ]
+        if last:
+            return part, copies2
+        cbuf[s, tp] = jnp.concatenate(part, axis=0).astype(BF16)
+        copies3 = tp_copies(s)
+        for copy in copies3:
+            copy.start()
+        for copy in copies2:
             copy.wait_send()
+        for copy in copies3:
+            copy.wait_recv()
+        total = (cbuf[s, 0].astype(F32) + cbuf[s, 1].astype(F32)) + (
+            cbuf[s, 2].astype(F32) + cbuf[s, 3].astype(F32)
+        )
+        hid[:, 0:640] = hid[:, 0:640] + total[0:8]
+        hid[:, 640:] = hid[:, 640:] + total[8:16]
         return 0
 
-    lax.fori_loop(0, STEPS, decode_step, 0)
-
+    lax.fori_loop(0, STEPS - 1, decode_step, 0)
+    part, pending = decode_step(STEPS - 1, 0, last=True)
+    for half in range(2):
+        cols = slice(half * 640, (half + 1) * 640)
+        value = part[half] + jnp.where(tp == 0, hid[:, cols], 0.0)
+        for i in range(4):
+            fsrc[i, :, cols] = value[2 * i : 2 * i + 2]
+    final = [
+        send(
+            fsrc.at[(g + dg) % 4], fbuf.at[g, tp],
+            fs_s.at[dg, dt], fs_r.at[dg, dt], at_both(dg, dt),
+        )
+        for dg in (2, 1, 3, 0) for dt in (2, 3, 1, 0) if dg + dt > 0
+    ]
+    for copy in final:
+        copy.start()
+    fbuf[g, tp] = fsrc[g]
+    store.wait()
+    for copy in sent + pending:
+        copy.wait_send()
+    for s in range(STEPS - 1):
+        for copy in tp_copies(s):
+            copy.wait_send()
+    for copy in final:
+        copy.wait()
     for i in range(4):
-        fsrc[i] = hid[2 * i : 2 * i + 2, :]
-    last = [
-        go(send(fsrc.at[(g + d) % 4], fbuf.at[g], fs_s.at[d - 1], fs_r.at[d - 1], at_g(d)))
-        for d in (1, 2, 3)
-    ]
-    fbuf[g] = fsrc[g]
-    for copy in last:
-        copy.wait_recv()
-    for i in range(4):
-        out_ref[:, i * BLK : (i + 1) * BLK] = fbuf[i].astype(BF16)
-    store.wait()
-    for copy in sent:
-        copy.wait_send()
+        out_ref[:, i * BLK : (i + 1) * BLK] = (
+            (fbuf[i, 0] + fbuf[i, 1]) + (fbuf[i, 2] + fbuf[i, 3])
+        ).astype(BF16)
 
 
 def on_device(
@@ -433,7 +466,7 @@
         scratch_shapes=[
             V((TOK, BLK), BF16), V((TOK, BLK), BF16), V((BLK, TOK), BF16),
             V((4, 4, SH, BLK), BF16), V((BLK, BLK), BF16),
-            V((CHUNKS, 6, 4, SH, HW), BF16), V((CHUNKS, 3, SH, CW), BF16),
+            V((CHUNKS, 6, 2, SH, CW), BF16), V((CHUNKS, 3, SH, CW), BF16),
             V((CHUNKS, 4, SH, CW), BF16),
             V((SH, BLK), F32), V((SH, BLK), F32), V((SH, BLK), F32), V((SH, BLK), F32),
             V((4, 2, BLK), F32), V((4, 2, BLK), F32),
@@ -442,13 +475,13 @@
             V((8, BLK), F32), V((2, 16, BLK), F32),
             V((STEPS, 4, 2, QW), F32), V((STEPS, 3, 2, QW), F32),
             V((STEPS, 4, 2, BLK), F32), V((8, BLK), F32),
-            V((STEPS, 2, 4, 8, 640), F32), V((4, 2, BLK), F32), V((4, 2, BLK), F32),
+            V((STEPS, 4, 16, 640), BF16), V((4, 2, BLK), F32), V((4, 4, 2, BLK), F32),
             dma((10,)),
             dma((CHUNKS, 6)), dma((CHUNKS, 6)), dma((CHUNKS, 3)), dma((CHUNKS, 3)),
             dma((CHUNKS, 3)), dma((CHUNKS, 3)), dma((CHUNKS, 4)), dma((CHUNKS, 4)),
             dma((3,)), dma((3,)), dma((STEPS, 3)), dma((STEPS, 3)),
-            dma((STEPS, 3)), dma((STEPS, 3)), dma((STEPS, 2, 3)), dma((STEPS, 2, 3)),
-            dma((3,)), dma((3,)),
+            dma((STEPS, 3)), dma((STEPS, 3)), dma((STEPS, 3)), dma((STEPS, 3)),
+            dma((4, 4)), dma((4, 4)),
         ],
         compiler_params=pltpu.CompilerParams(
             collective_id=0, has_side_effects=True, vmem_limit_bytes=56 * 1024 * 1024

time: 145 us -> 139 us (0.959)
  Pallas kernels: 144 us -> 138 us
    pallas_call x1, Pallas kernels: 141 us -> 136 us  [on_device(): pl.pallas_call(kernel, out_shape=(shard, rows), in_specs=[hbm, hbm] + [vm...]
where the time goes in v3:
time: 139 us
  Pallas kernels  138 us (99%)
    pallas_call x1, Pallas kernels, on_device(): pl.pallas_call(kernel, out_shape=(shard, rows), in_specs=[hbm, hbm] + [vm...  136 us

profile of v3, /device:TPU:1, one launch (start us, length us, event | category | flops | bytes accessed | tf_op | source)
XLA Modules:
  0.0 138.6 jit_solution(1768590295783806978)
XLA Ops:
  0.6 135.5 %shard_map.174 = (f32[80,1280]{1,0:T(8,128)}, bf16[2,5120]{1,0:T(2,128)(2,1)}) custom-call(bf16[1024,1280]{1,0:T(8,128)(2,1)} %inp_h.1, bf16[1024,1280]{1,0:T(8,128)(2,1)} %cot_h.1, s32[8,128]{1,0:T(8,128)} %bitcast.5, f32[1,64]{1,0:T(1,128)} %bitcast.6, s32[1,64]{1,0:T(1,128)} %bitcast.7, f32[80,1280]{1,0:T(8,128)} %master.1, f32[80,1280]{1,0:T(8,128)} %first.1, ...), custom_call_target="tpu_custom_call" | custom-call | tf_op jit(solution)/shard_map/pallas_call | solution.py:461
  136.1 2.5 %shard_map.175 = (f32[80,1280]{1,0:T(8,128)}, f32[80,1280]{1,0:T(8,128)}, f32[80,1280]{1,0:T(8,128)}, bf16[2,5120]{1,0:T(2,128)(2,1)}) custom-call(f32[80,1280]{1,0:T(8,128)} %get-tuple-element.6.grad, f32[80,1280]{1,0:T(8,128)} %master.1, f32[80,1280]{1,0:T(8,128)} %first.1, f32[80,1280]{1,0:T(8,128)} %second.1, bf16[2,5120]{1,0:T(2,128)(2,1)} %get-tuple-element.7.rows), custom_call_target="tpu_custom_call" | custom-call | tf_op jit(solution)/shard_map/pallas_call | solution.py:497

commit v4 on v3

--- a/solution.py
+++ b/solution.py
@@ -70,20 +70,25 @@
     tp = lax.axis_index("tp")
     z, y = fs // 4, fs % 4
 
+    y_ids = [(z * 4 + (y + d) % 4, g, tp) for d in range(4)]
+    z_ids = [(((z + d) % 4) * 4 + y, g, tp) for d in range(4)]
+    g_at = [(g + d) % 4 for d in range(4)]
+    tp_at = [(tp + d) % 4 for d in range(4)]
+
     def at_y(d):
-        return {"fsdp": z * 4 + (y + d) % 4}
+        return y_ids[d]
 
     def at_z(d):
-        return {"fsdp": ((z + d) % 4) * 4 + y}
+        return z_ids[d]
 
     def at_g(d):
-        return {"grp": (g + d) % 4}
+        return fs, g_at[d], tp
+
+    def at_tp(d):
+        return fs, g, tp_at[d]
 
     def at_both(dg, dt):
-        return {"grp": (g + dg) % 4, "tp": (tp + dt) % 4}
-
-    def at_tp(d):
-        return {"tp": (tp + d) % 4}
+        return fs, g_at[dg], tp_at[dt]
 
     def send(src, dst, ssem, rsem, where):
         return pltpu.make_async_remote_copy(
@@ -260,7 +265,7 @@
     gradient_chunk(0)
     pl.semaphore_wait(barrier, len(greeted))
     for t in range(LAG[-1] + CHUNKS):
-        for stage, lag in zip(stages, LAG):
+        for stage, lag in list(zip(stages, LAG))[1:] + [(reduce_a, 0)]:
             if 0 <= t - lag < CHUNKS:
                 stage(t - lag)
         if t == 0:

time: 139 us -> 138 us (level)
  no operation moved by 1% of the time
where the time goes in v4:
time: 138 us
  Pallas kernels  137 us (99%)
    pallas_call x1, Pallas kernels, on_device(): pl.pallas_call(kernel, out_shape=(shard, rows), in_specs=[hbm, hbm] + [vm...  134 us

profile of v4, /device:TPU:1, one launch (start us, length us, event | category | flops | bytes accessed | tf_op | source)
XLA Modules:
  0.0 137.6 jit_solution(16411845476117525315)
XLA Ops:
  0.6 134.5 %shard_map.174 = (f32[80,1280]{1,0:T(8,128)}, bf16[2,5120]{1,0:T(2,128)(2,1)}) custom-call(bf16[1024,1280]{1,0:T(8,128)(2,1)} %inp_h.1, bf16[1024,1280]{1,0:T(8,128)(2,1)} %cot_h.1, s32[8,128]{1,0:T(8,128)} %bitcast.5, f32[1,64]{1,0:T(1,128)} %bitcast.6, s32[1,64]{1,0:T(1,128)} %bitcast.7, f32[80,1280]{1,0:T(8,128)} %master.1, f32[80,1280]{1,0:T(8,128)} %first.1, ...), custom_call_target="tpu_custom_call" | custom-call | tf_op jit(solution)/shard_map/pallas_call | solution.py:466
  135.1 2.5 %shard_map.175 = (f32[80,1280]{1,0:T(8,128)}, f32[80,1280]{1,0:T(8,128)}, f32[80,1280]{1,0:T(8,128)}, bf16[2,5120]{1,0:T(2,128)(2,1)}) custom-call(f32[80,1280]{1,0:T(8,128)} %get-tuple-element.6.grad, f32[80,1280]{1,0:T(8,128)} %master.1, f32[80,1280]{1,0:T(8,128)} %first.1, f32[80,1280]{1,0:T(8,128)} %second.1, bf16[2,5120]{1,0:T(2,128)(2,1)} %get-tuple-element.7.rows), custom_call_target="tpu_custom_call" | custom-call | tf_op jit(solution)/shard_map/pallas_call | solution.py:502

commit v5 on v4

--- a/solution.py
+++ b/solution.py
@@ -22,6 +22,7 @@
 TOK = 1024
 CW = 128
 CHUNKS = BLK // CW
+EARLY = BLK - 2 * CW
 LAG = (0, 2, 4, 6, 8, 10, 12)
 LC = 128
 HEADS = BLK // HEAD
@@ -61,7 +62,7 @@
     gout_h, out_ref,
     inp, cot, sigt, grad, wblk, ry, rz, zacc,
     wm, m1, m2, gsum, hsrc, hbuf, ck, cv, st, sw, dec,
-    hid, own, qsend, qrecv, mixbuf, mix8, cbuf, fsrc, fbuf,
+    hid, qacc, own, qsend, qrecv, mixbuf, mix8, cbuf, fsrc, fbuf,
     lsem, ysend, yrecv, zsend, zrecv, azs, azr, ays, ayr,
     hs_s, hs_r, qs_s, qs_r, ms_s, ms_r, cs_s, cs_r, fs_s, fs_r,
 ):
@@ -262,23 +263,64 @@
         send(hsrc.at[(g + d) % 4], hbuf.at[g], hs_s.at[d - 1], hs_r.at[d - 1], at_g(d))
         for d in (1, 2, 3)
     ]
+    def halves():
+        h = hid[...]
+        high = h.astype(BF16).astype(F32)
+        return h, jnp.concatenate([high, h - high], axis=0).astype(BF16)
+
+    def project(both, n, left, right):
+        return lax.dot_general(
+            both[:, left:right], wblk[n * 256 : (n + 1) * 256, left:right], NT,
+            preferred_element_type=F32,
+        )
+
+    def put(s, part, left, right):
+        part = part[0:8] + part[8:16]
+        for i in range(4):
+            qsend[s, i, :, left:right] = part[2 * i : 2 * i + 2]
+
+    def gates_of(s, h, both):
+        put(s, jnp.dot(both, sw[...], preferred_element_type=F32), BLK, BLK + 2 * NST)
+        square = jnp.broadcast_to(jnp.sum(h * h, axis=1, keepdims=True), (8, 128))
+        for i in range(4):
+            qsend[s, i, :, BLK + 2 * NST :] = square[2 * i : 2 * i + 2]
+
+    def query_of(s):
+        h, both = halves()
+        for n in range(BLK // 256):
+            put(s, project(both, n, 0, BLK), n * 256, (n + 1) * 256)
+        gates_of(s, h, both)
+
+    def first_query():
+        for copy in hcopies:
+            copy.wait()
+        for i in range(4):
+            hid[2 * i : 2 * i + 2, :] = hbuf[i]
+        for copy in loads[5:]:
+            copy.wait()
+
+        h, both = halves()
+        gates_of(0, h, both)
+        for n in range(BLK // 256):
+            qacc[:, n * 256 : (n + 1) * 256] = project(both, n, 0, EARLY)
+
     gradient_chunk(0)
     pl.semaphore_wait(barrier, len(greeted))
     for t in range(LAG[-1] + CHUNKS):
         for stage, lag in list(zip(stages, LAG))[1:] + [(reduce_a, 0)]:
             if 0 <= t - lag < CHUNKS:
                 stage(t - lag)
+        if t == LAG[-1] + CHUNKS - 3:
+            first_query()
         if t == 0:
             for copy in hcopies:
                 copy.start()
             hbuf[g] = hsrc[g]
 
-    for copy in hcopies:
-        copy.wait()
-    for i in range(4):
-        hid[2 * i : 2 * i + 2, :] = hbuf[i]
-    for copy in loads[5:]:
-        copy.wait()
+    _, both = halves()
+    for n in range(BLK // 256):
+        cols = slice(n * 256, (n + 1) * 256)
+        put(0, qacc[:, cols] + project(both, n, EARLY, BLK), n * 256, (n + 1) * 256)
 
     head_of = (
         lax.broadcasted_iota(jnp.int32, (16, BLK), 1) // HEAD
@@ -298,22 +340,6 @@
         ]
 
     def decode_step(s, _, last=False):
-        h = hid[...]
-        high = h.astype(BF16).astype(F32)
-        both = jnp.concatenate([high, h - high], axis=0).astype(BF16)
-        for n in range(BLK // 256):
-            part = lax.dot_general(
-                both, wblk[n * 256 : (n + 1) * 256, :], NT, preferred_element_type=F32
-            )
-            part = part[0:8] + part[8:16]
-            for i in range(4):
-                qsend[s, i, :, n * 256 : (n + 1) * 256] = part[2 * i : 2 * i + 2]
-        part = jnp.dot(both, sw[...], preferred_element_type=F32)
-        part = part[0:8] + part[8:16]
-        square = jnp.broadcast_to(jnp.sum(h * h, axis=1, keepdims=True), (8, 128))
-        for i in range(4):
-            qsend[s, i, :, BLK : BLK + 2 * NST] = part[2 * i : 2 * i + 2]
-            qsend[s, i, :, BLK + 2 * NST :] = square[2 * i : 2 * i + 2]
         copies = [
             send(
                 qsend.at[s, (g + d) % 4], qrecv.at[s, d - 1],
@@ -418,6 +444,7 @@
         )
         hid[:, 0:640] = hid[:, 0:640] + total[0:8]
         hid[:, 640:] = hid[:, 640:] + total[8:16]
+        query_of(s + 1)
         return 0
 
     lax.fori_loop(0, STEPS - 1, decode_step, 0)
@@ -477,7 +504,7 @@
             V((4, 2, BLK), F32), V((4, 2, BLK), F32),
             V((2, LC, BLK), BF16), V((2, LC, BLK), BF16), V((2, NST, BLK), F32),
             V((BLK, 2 * NST), BF16), V((1, BLK), F32),
-            V((8, BLK), F32), V((2, 16, BLK), F32),
+            V((8, BLK), F32), V((16, BLK), F32), V((2, 16, BLK), F32),
             V((STEPS, 4, 2, QW), F32), V((STEPS, 3, 2, QW), F32),
             V((STEPS, 4, 2, BLK), F32), V((8, BLK), F32),
             V((STEPS, 4, 16, 640), BF16), V((4, 2, BLK), F32), V((4, 4, 2, BLK), F32),
@@ -497,11 +524,11 @@
         cache_keys, cache_values, cache_lengths, ssm_state, state_weight,
         decay_rate.reshape(HEADS, 128),
     )
-    part = pl.BlockSpec((SH, BLK // 2), lambda i: (0, i))
+    part = pl.BlockSpec((SH, BLK), lambda i: (0, i))
     whole = pl.BlockSpec((2, D), lambda i: (0, 0))
     return pl.pallas_call(
         finish,
-        grid=(2,),
+        grid=(1,),
         out_shape=(shard, shard, shard, rows),
         in_specs=[part] * 4 + [whole],
         out_specs=(part, part, part, whole),

time: 138 us -> 138 us (level)
  no operation moved by 1% of the time
where the time goes in v5:
time: 138 us; the launch traced here: 137 us
  Pallas kernels  136 us (99%)
    pallas_call x1, Pallas kernels, on_device(): pl.pallas_call(kernel, out_shape=(shard, rows), in_specs=[hbm, hbm] + [vm...  134 us

profile of v5, /device:TPU:1, one launch (start us, length us, event | category | flops | bytes accessed | tf_op | source)
XLA Modules:
  0.0 137.0 jit_solution(15316253498207222655)
XLA Ops:
  0.6 133.7 %shard_map.174 = (f32[80,1280]{1,0:T(8,128)}, bf16[2,5120]{1,0:T(2,128)(2,1)}) custom-call(bf16[1024,1280]{1,0:T(8,128)(2,1)} %inp_h.1, bf16[1024,1280]{1,0:T(8,128)(2,1)} %cot_h.1, s32[8,128]{1,0:T(8,128)} %bitcast.5, f32[1,64]{1,0:T(1,128)} %bitcast.6, s32[1,64]{1,0:T(1,128)} %bitcast.7, f32[80,1280]{1,0:T(8,128)} %master.1, f32[80,1280]{1,0:T(8,128)} %first.1, ...), custom_call_target="tpu_custom_call" | custom-call | tf_op jit(solution)/shard_map/pallas_call | solution.py:493
  134.4 2.7 %shard_map.175 = (f32[80,1280]{1,0:T(8,128)}, f32[80,1280]{1,0:T(8,128)}, f32[80,1280]{1,0:T(8,128)}, bf16[2,5120]{1,0:T(2,128)(2,1)}) custom-call(f32[80,1280]{1,0:T(8,128)} %get-tuple-element.6.grad, f32[80,1280]{1,0:T(8,128)} %master.1, f32[80,1280]{1,0:T(8,128)} %first.1, f32[80,1280]{1,0:T(8,128)} %second.1, bf16[2,5120]{1,0:T(2,128)(2,1)} %get-tuple-element.7.rows), custom_call_target="tpu_custom_call" | custom-call | tf_op jit(solution)/shard_map/pallas_call | solution.py:529
